TPU v7x, 512 devices: a whole 4x4x16 slice. The times are simulated.
512 devices in a mesh: rows: 8 (over y, x_lo), cols: 64 (over x_hi, z, core).
Axes of the slice: x: 4 (x_hi: 2, x_lo: 2; x = x_hi * 2 + x_lo), y: 4, z: 16, core: 2. Of those that a mesh axis runs over, the one named last changes fastest.
Arguments:
- fine_in: bfloat16 [64, 4096, 256], P('rows', 'cols'), may hold values from -6 to 6
- mid_in: bfloat16 [32, 2048, 256], P('rows', 'cols'), may hold values from -6 to 6
- coarse_in: bfloat16 [16, 1024, 256], P('rows', 'cols'), may hold values from -6 to 6
- lateral_weight: bfloat16 [768, 256], replicated, may hold values from -0.375 to 0.375
- out_weight: bfloat16 [2304, 256], replicated, may hold values from -0.125 to 0.125
- cotangent: bfloat16 [64, 4096, 256], P('rows', 'cols'), may hold values from -6 to 6
Outputs:
- mask_features: bfloat16 [64, 4096, 256], P('rows', 'cols')
- fine_grad: bfloat16 [64, 4096, 256], P('rows', 'cols')
- mid_grad: bfloat16 [32, 2048, 256], P('rows', 'cols')
- coarse_grad: bfloat16 [16, 1024, 256], P('rows', 'cols')
- lateral_grad: float32 [768, 256], P('cols', 'rows')
- conv_grad: float32 [2304, 256], P('cols', 'rows')
All inputs are finite; a program needn't handle non-finite values.
Results may differ from a plain program's by a relative error of at most 0.017.
Values may be sent and summed in bfloat16 or wider, within the bound.
A program may use at most 64 MiB of HBM per device.

v0:
```python
import jax
import jax.numpy as jnp
from jax import lax
from jax.sharding import PartitionSpec as P


def extended(cells, sides, width):
    for axis, dim in sides:
        count = lax.axis_size(axis)
        ends = count - 1
        head = lax.slice_in_dim(cells, 0, width, axis=dim)
        tail = lax.slice_in_dim(cells, cells.shape[dim] - width, cells.shape[dim], axis=dim)
        cells = jnp.concatenate(
            [
                lax.ppermute(tail, axis, [(i, (i + 1) % count) for i in range(ends)]),
                cells,
                lax.ppermute(head, axis, [((i + 1) % count, i) for i in range(ends)]),
            ],
            axis=dim,
        )
    return cells


def lateral(feature, weight):
    height, width, chans = feature.shape
    flat = jnp.dot(
        feature.reshape(height * width, chans), weight, preferred_element_type=jnp.float32
    )
    return flat.reshape(height, width, weight.shape[1])


def outer(left, right):
    chans = left.shape[-1]
    return lax.dot_general(
        left.reshape(-1, chans),
        right.reshape(-1, right.shape[-1]),
        (((0,), (0,)), ((), ())),
        preferred_element_type=jnp.float32,
    )


def widen(coarse, axis):
    count = coarse.shape[axis] - 2
    lower = lax.slice_in_dim(coarse, 0, count, axis=axis)
    middle = lax.slice_in_dim(coarse, 1, count + 1, axis=axis)
    upper = lax.slice_in_dim(coarse, 2, count + 2, axis=axis)
    even = 0.25 * lower + 0.75 * middle
    odd = 0.75 * middle + 0.25 * upper
    joined = jnp.stack([even, odd], axis=axis + 1)
    shape = list(coarse.shape)
    shape[axis] = 2 * count
    return joined.reshape(shape)


def narrow(fine, axis):
    total = fine.shape[axis] - 2
    count = total // 2
    prior_tensor = lax.slice_in_dim(fine, 0, total, axis=axis)
    inner = lax.slice_in_dim(fine, 1, total + 1, axis=axis)
    after = lax.slice_in_dim(fine, 2, total + 2, axis=axis)
    shape = fine.shape[:axis] + (count, 2) + fine.shape[axis + 1 :]
    prior_tensor = prior_tensor.reshape(shape)
    inner = inner.reshape(shape)
    after = after.reshape(shape)
    return (
        0.25 * lax.index_in_dim(prior_tensor, 0, axis + 1, keepdims=False)
        + 0.75 * lax.index_in_dim(inner, 0, axis + 1, keepdims=False)
        + 0.75 * lax.index_in_dim(inner, 1, axis + 1, keepdims=False)
        + 0.25 * lax.index_in_dim(after, 1, axis + 1, keepdims=False)
    )


def border_limiter(padded):
    at_top = lax.axis_index("rows") == 0
    at_bottom = lax.axis_index("rows") == lax.axis_size("rows") - 1
    first = jnp.where(at_top, padded[1:2], padded[0:1])
    last = jnp.where(at_bottom, padded[-2:-1], padded[-1:])
    padded = jnp.concatenate([first, padded[1:-1], last], 0)
    at_left = lax.axis_index("cols") == 0
    at_right = lax.axis_index("cols") == lax.axis_size("cols") - 1
    first = jnp.where(at_left, padded[:, 1:2], padded[:, 0:1])
    last = jnp.where(at_right, padded[:, -2:-1], padded[:, -1:])
    return jnp.concatenate([first, padded[:, 1:-1], last], 1)


def extend(receptive_region, clamped):
    padded = extended(receptive_region, (("rows", 0), ("cols", 1)), 1)
    if clamped:
        padded = border_limiter(padded)
    return padded


def upsample(receptive_region):
    return widen(widen(extend(receptive_region, True).astype(jnp.float32), 0), 1)


def reduce_resolution(receptive_region):
    return narrow(narrow(extend(receptive_region, True).astype(jnp.float32), 0), 1)


def gather_taps(padded, height, width, flipped):
    pieces = []
    for tap in range(9):
        row_off, col_off = divmod(tap, 3)
        if flipped:
            row_off, col_off = (2 - row_off, 2 - col_off)
        pieces.append(padded[row_off : row_off + height, col_off : col_off + width])
    joined = jnp.concatenate(pieces, -1)
    return joined.reshape(height * width, joined.shape[-1])


def gelu_exact(value):
    return jax.nn.gelu(value, approximate=False)


def local(fine_in, mid_in, coarse_in, lateral_weight, out_weight, cotangent):
    height, width, chans = fine_in.shape
    w_fine = lateral_weight[0:chans]
    w_mid = lateral_weight[chans : 2 * chans]
    w_top = lateral_weight[2 * chans : 3 * chans]
    top = lateral(coarse_in, w_top).astype(jnp.bfloat16)
    middle = (lateral(mid_in, w_mid) + upsample(top)).astype(jnp.bfloat16)
    fine = (lateral(fine_in, w_fine) + upsample(middle)).astype(jnp.bfloat16)
    window_tiles = gather_taps(extend(fine, False), height, width, False)
    pre = jnp.dot(window_tiles, out_weight, preferred_element_type=jnp.float32)
    outputs, pull = jax.vjp(gelu_exact, pre)
    mask_features = outputs.astype(jnp.bfloat16).reshape(height, width, chans)
    dpre = pull(cotangent.reshape(height * width, chans).astype(jnp.float32))[0].astype(
        jnp.bfloat16
    )
    dpre_field = dpre.reshape(height, width, chans)
    back_patches = gather_taps(extend(dpre_field, False), height, width, True)
    turned = jnp.transpose(out_weight.reshape(9, chans, chans), (0, 2, 1)).reshape(9 * chans, chans)
    fine_level_grad = jnp.dot(back_patches, turned, preferred_element_type=jnp.float32).astype(
        jnp.bfloat16
    )
    fine_level_grad = fine_level_grad.reshape(height, width, chans)
    conv_terms = lax.dot_general(
        window_tiles, dpre, (((0,), (0,)), ((), ())), preferred_element_type=jnp.float32
    )
    middle_level_grad = reduce_resolution(fine_level_grad).astype(jnp.bfloat16)
    top_level_grad = reduce_resolution(middle_level_grad).astype(jnp.bfloat16)
    fine_grad = lateral(fine_level_grad, w_fine.T).astype(jnp.bfloat16)
    mid_grad = lateral(middle_level_grad, w_mid.T).astype(jnp.bfloat16)
    coarse_grad = lateral(top_level_grad, w_top.T).astype(jnp.bfloat16)
    lateral_terms = jnp.concatenate(
        [
            outer(fine_in, fine_level_grad),
            outer(mid_in, middle_level_grad),
            outer(coarse_in, top_level_grad),
        ],
        0,
    )
    lateral_part, conv_part = (
        lax.psum_scatter(lateral_terms, "cols", scatter_dimension=0, tiled=True),
        lax.psum_scatter(conv_terms, "cols", scatter_dimension=0, tiled=True),
    )
    lateral_grad, conv_grad = (
        lax.psum_scatter(
            lateral_part.astype(jnp.bfloat16), "rows", scatter_dimension=1, tiled=True
        ).astype(jnp.float32),
        lax.psum_scatter(
            conv_part.astype(jnp.bfloat16), "rows", scatter_dimension=1, tiled=True
        ).astype(jnp.float32),
    )
    return (mask_features, fine_grad, mid_grad, coarse_grad, lateral_grad, conv_grad)


def solution(mesh):
    in_specs = (
        P("rows", "cols", None),
        P("rows", "cols", None),
        P("rows", "cols", None),
        P(),
        P(),
        P("rows", "cols", None),
    )
    out_specs = (
        P("rows", "cols", None),
        P("rows", "cols", None),
        P("rows", "cols", None),
        P("rows", "cols", None),
        P("cols", "rows"),
        P("cols", "rows"),
    )
    return jax.shard_map(local, mesh=mesh, in_specs=in_specs, out_specs=out_specs, check_vma=False)
```

profile of v0, /device:TPU:1, one launch (start us, length us, event | category | flops | bytes accessed | tf_op | source)
XLA Modules:
  0.0 474.5 jit_solution(5557376299334431318)
XLA Ops:
  9.7 4.6 collective-permute-start
  15.0 9.3 %collective-permute-start.3 = (bf16[4,1,256]{2,1,0:T(2,128)(2,1)S(1)}, bf16[4,1,256]{2,1,0:T(2,128)(2,1)S(1)}, u32[]{:S(2)}, u32[]{:S(2)}) collective-permute-start(bf16[4,1,256]{2,1,0:T(2,128)(2,1)S(1)} %get-tuple-element.109), channel_id=1, source_target_pairs={{1,0},{2,1},{3,2},{4,3},{5,4},{6,5},{7,6},{8,7},{9,8},{10,9},{11,1... | collective-permute-start | bytes 6152 | tf_op jit(solution)/shard_map/ppermute | solution.py:17
  29.6 4.5 collective-permute-start.4
  35.0 2.9 collective-permute-start.7
  37.9 3.6 collective-permute-start.6
  45.5 5.2 %collective-permute-start.8 = (bf16[1,64,256]{2,1,0:T(8,128)(2,1)S(1)}, bf16[1,64,256]{2,1,0:T(8,128)(2,1)S(1)}, u32[]{:S(2)}, u32[]{:S(2)}) collective-permute-start(bf16[1,64,256]{2,1,0:T(8,128)(2,1)S(1)} %get-tuple-element.70), channel_id=1, source_target_pairs={{0,64},{64,128},{128,192},{192,256},{256,320},{320,384},{384,448},... | collective-permute-start | bytes 98312 | tf_op jit(solution)/shard_map/ppermute | solution.py:15
  53.6 5.1 %collective-permute-start.10 = (bf16[10,1,256]{2,1,0:T(2,128)(2,1)S(1)}, bf16[10,1,256]{2,1,0:T(2,128)(2,1)S(1)}, u32[]{:S(2)}, u32[]{:S(2)}) collective-permute-start(bf16[10,1,256]{2,1,0:T(2,128)(2,1)S(1)} %get-tuple-element.56), channel_id=1, source_target_pairs={{0,1},{1,2},{2,3},{3,4},{4,5},{5,6},{6,7},{7,8},{8,9},{9,10},{10,1... | collective-permute-start | bytes 15368 | tf_op jit(solution)/shard_map/ppermute | solution.py:15
  65.1 5.4 %collective-permute-start.12 = (bf16[1,64,256]{2,1,0:T(8,128)(2,1)S(1)}, bf16[1,64,256]{2,1,0:T(8,128)(2,1)S(1)}, u32[]{:S(2)}, u32[]{:S(2)}) collective-permute-start(bf16[1,64,256]{2,1,0:T(8,128)(2,1)S(1)} %get-tuple-element.68), channel_id=1, source_target_pairs={{0,64},{64,128},{128,192},{192,256},{256,320},{320,384},{384,448},... | collective-permute-start | bytes 98312 | tf_op jit(solution)/shard_map/ppermute | solution.py:15
  71.5 5.0 %collective-permute-start.15 = (bf16[10,1,256]{2,1,0:T(2,128)(2,1)S(1)}, bf16[10,1,256]{2,1,0:T(2,128)(2,1)S(1)}, u32[]{:S(2)}, u32[]{:S(2)}) collective-permute-start(bf16[10,1,256]{2,1,0:T(2,128)(2,1)S(1)} %get-tuple-element.51), channel_id=1, source_target_pairs={{0,1},{1,2},{2,3},{3,4},{4,5},{5,6},{6,7},{7,8},{8,9},{9,10},{10,1... | collective-permute-start | bytes 15368 | tf_op jit(solution)/shard_map/ppermute | solution.py:15
  78.6 3.0 collective-permute-done.14
  84.3 5.5 %collective-permute-start.16 = (bf16[1,64,256]{2,1,0:T(8,128)(2,1)S(1)}, bf16[1,64,256]{2,1,0:T(8,128)(2,1)S(1)}, u32[]{:S(2)}, u32[]{:S(2)}) collective-permute-start(bf16[1,64,256]{2,1,0:T(8,128)(2,1)S(1)} %get-tuple-element.64), channel_id=1, source_target_pairs={{0,64},{64,128},{128,192},{192,256},{256,320},{320,384},{384,448},... | collective-permute-start | bytes 98312 | tf_op jit(solution)/shard_map/ppermute | solution.py:15
  92.7 3.8 collective-permute-start.18
  110.6 5.5 %collective-permute-start.20 = (bf16[1,32,256]{2,1,0:T(8,128)(2,1)S(1)}, bf16[1,32,256]{2,1,0:T(8,128)(2,1)S(1)}, u32[]{:S(2)}, u32[]{:S(2)}) collective-permute-start(bf16[1,32,256]{2,1,0:T(8,128)(2,1)S(1)} %get-tuple-element.94), channel_id=1, source_target_pairs={{0,64},{64,128},{128,192},{192,256},{256,320},{320,384},{384,448},... | collective-permute-start | bytes 49160 | tf_op jit(solution)/shard_map/ppermute | solution.py:15
  118.9 4.8 %collective-permute-start.22 = (bf16[6,1,256]{2,1,0:T(2,128)(2,1)S(1)}, bf16[6,1,256]{2,1,0:T(2,128)(2,1)S(1)}, u32[]{:S(2)}, u32[]{:S(2)}) collective-permute-start(bf16[6,1,256]{2,1,0:T(2,128)(2,1)S(1)} %get-tuple-element.83), channel_id=1, source_target_pairs={{0,1},{1,2},{2,3},{3,4},{4,5},{5,6},{6,7},{7,8},{8,9},{9,10},{10,1... | collective-permute-start | bytes 9224 | tf_op jit(solution)/shard_map/ppermute | solution.py:15
  125.4 150.6 %fusion.66 = (f32[16,256]{1,0:T(8,128)S(1)}, f32[40,256]{1,0:T(8,128)S(1)}) fusion(f32[768,256]{1,0:T(8,128)S(1)} %pad_maximum_fusion, f32[2304,256]{1,0:T(8,128)S(1)} %fusion.81), kind=kCustom, calls=%all-reduce-scatter.2 | all-reduce-scatter fusion | flops 917506 | bytes 3205120
  277.3 36.8 %collective-permute-start.37 = (bf16[16,256]{1,0:T(8,128)(2,1)S(1)}, bf16[16,256]{1,0:T(8,128)(2,1)S(1)}, u32[]{:S(2)}, u32[]{:S(2)}) collective-permute-start(bf16[16,256]{1,0:T(8,128)(2,1)S(1)} %convert.75), channel_id=1, source_target_pairs={{0,14},{1,15},{2,16},{3,17},{4,18},{5,19},{6,20},{7,21},{8,22},{9,... | collective-permute-start | bytes 24584
  314.1 8.8 %collective-permute-start.39 = (bf16[12,256]{1,0:T(8,128)(2,1)S(1)}, bf16[12,256]{1,0:T(8,128)(2,1)S(1)}, u32[]{:S(2)}, u32[]{:S(2)}) collective-permute-start(bf16[12,256]{1,0:T(8,128)(2,1)S(1)} %slice.608), channel_id=1, source_target_pairs={{0,16},{1,17},{2,18},{3,19},{4,20},{5,21},{6,22},{7,23},{8,24},{9,... | collective-permute-start | bytes 18440
  328.8 4.2 collective-permute-start.33
  333.0 7.2 %collective-permute-start.32 = (bf16[16,256]{1,0:T(8,128)(2,1)S(1)}, bf16[16,256]{1,0:T(8,128)(2,1)S(1)}, u32[]{:S(2)}, u32[]{:S(2)}) collective-permute-start(bf16[16,256]{1,0:T(8,128)(2,1)S(1)} %convert.75), channel_id=1, source_target_pairs={{0,9},{1,10},{2,11},{3,12},{4,13},{5,14},{6,15},{7,16},{8,17},{9,1... | collective-permute-start | bytes 24584
  342.2 3.3 collective-permute-start.31
  348.2 4.2 collective-permute-start.29
  367.2 4.5 collective-permute-start.45
  391.0 28.9 %reduce-scatter.11.cloned.1.call-done = bf16[32,12]{1,0:T(8,128)(2,1)} async-done(((bf16[256,12]{1,0:T(8,128)(2,1)}), bf16[32,12]{1,0:T(8,128)(2,1)}) %reduce-scatter.11.cloned.1.call-update) | async-done | bytes 784
  421.3 44.9 %reduce-scatter.13.cloned.1.call-done = bf16[32,36]{1,0:T(8,128)(2,1)} async-done(((bf16[256,36]{1,0:T(8,128)(2,1)}), bf16[32,36]{1,0:T(8,128)(2,1)}) %reduce-scatter.13.cloned.1.call-update) | async-done | bytes 2320
  (227 shorter events, 96.6 us)
Async XLA Ops:
  7.2 412.7 %reduce-scatter.11.cloned.1.call-start = ((), (), s32[]{:S(2)}) async-start(), calls=%async_computation.2 | async-start | bytes 73728
  15.0 11.3 %collective-permute-start.3 = (bf16[4,1,256]{2,1,0:T(2,128)(2,1)S(1)}, bf16[4,1,256]{2,1,0:T(2,128)(2,1)S(1)}, u32[]{:S(2)}, u32[]{:S(2)}) collective-permute-start(bf16[4,1,256]{2,1,0:T(2,128)(2,1)S(1)} %get-tuple-element.109), channel_id=1, source_target_pairs={{1,0},{2,1},{3,2},{4,3},{5,4},{6,5},{7,6},{8,7},{9,8},{10,9},{11,1... | collective-permute-start | bytes 6152 | tf_op jit(solution)/shard_map/ppermute | solution.py:17
  276.0 52.8 %collective-permute-start.38 = (bf16[16,256]{1,0:T(8,128)(2,1)S(1)}, bf16[16,256]{1,0:T(8,128)(2,1)S(1)}, u32[]{:S(2)}, u32[]{:S(2)}) collective-permute-start(bf16[16,256]{1,0:T(8,128)(2,1)S(1)} %convert.75), channel_id=1, source_target_pairs={{0,15},{1,16},{2,17},{3,18},{4,19},{5,20},{6,21},{7,22},{8,23},{9,... | collective-permute-start | bytes 24584
  277.3 55.6 %collective-permute-start.37 = (bf16[16,256]{1,0:T(8,128)(2,1)S(1)}, bf16[16,256]{1,0:T(8,128)(2,1)S(1)}, u32[]{:S(2)}, u32[]{:S(2)}) collective-permute-start(bf16[16,256]{1,0:T(8,128)(2,1)S(1)} %convert.75), channel_id=1, source_target_pairs={{0,14},{1,15},{2,16},{3,17},{4,18},{5,19},{6,20},{7,21},{8,22},{9,... | collective-permute-start | bytes 24584
  314.1 13.4 %collective-permute-start.39 = (bf16[12,256]{1,0:T(8,128)(2,1)S(1)}, bf16[12,256]{1,0:T(8,128)(2,1)S(1)}, u32[]{:S(2)}, u32[]{:S(2)}) collective-permute-start(bf16[12,256]{1,0:T(8,128)(2,1)S(1)} %slice.608), channel_id=1, source_target_pairs={{0,16},{1,17},{2,18},{3,19},{4,20},{5,21},{6,22},{7,23},{8,24},{9,... | collective-permute-start | bytes 18440
  324.9 17.3 %collective-permute-start.36 = (bf16[16,256]{1,0:T(8,128)(2,1)S(1)}, bf16[16,256]{1,0:T(8,128)(2,1)S(1)}, u32[]{:S(2)}, u32[]{:S(2)}) collective-permute-start(bf16[16,256]{1,0:T(8,128)(2,1)S(1)} %convert.75), channel_id=1, source_target_pairs={{0,13},{1,14},{2,15},{3,16},{4,17},{5,18},{6,19},{7,20},{8,21},{9,... | collective-permute-start | bytes 24584
  326.2 19.4 %collective-permute-start.35 = (bf16[16,256]{1,0:T(8,128)(2,1)S(1)}, bf16[16,256]{1,0:T(8,128)(2,1)S(1)}, u32[]{:S(2)}, u32[]{:S(2)}) collective-permute-start(bf16[16,256]{1,0:T(8,128)(2,1)S(1)} %convert.75), channel_id=1, source_target_pairs={{0,12},{1,13},{2,14},{3,15},{4,16},{5,17},{6,18},{7,19},{8,20},{9,... | collective-permute-start | bytes 24584
  327.5 20.7 %collective-permute-start.34 = (bf16[16,256]{1,0:T(8,128)(2,1)S(1)}, bf16[16,256]{1,0:T(8,128)(2,1)S(1)}, u32[]{:S(2)}, u32[]{:S(2)}) collective-permute-start(bf16[16,256]{1,0:T(8,128)(2,1)S(1)} %convert.75), channel_id=1, source_target_pairs={{0,11},{1,12},{2,13},{3,14},{4,15},{5,16},{6,17},{7,18},{8,19},{9,... | collective-permute-start | bytes 24584
  328.8 23.6 %collective-permute-start.33 = (bf16[16,256]{1,0:T(8,128)(2,1)S(1)}, bf16[16,256]{1,0:T(8,128)(2,1)S(1)}, u32[]{:S(2)}, u32[]{:S(2)}) collective-permute-start(bf16[16,256]{1,0:T(8,128)(2,1)S(1)} %convert.75), channel_id=1, source_target_pairs={{0,10},{1,11},{2,12},{3,13},{4,14},{5,15},{6,16},{7,17},{8,18},{9,... | collective-permute-start | bytes 24584
  333.0 21.3 %collective-permute-start.32 = (bf16[16,256]{1,0:T(8,128)(2,1)S(1)}, bf16[16,256]{1,0:T(8,128)(2,1)S(1)}, u32[]{:S(2)}, u32[]{:S(2)}) collective-permute-start(bf16[16,256]{1,0:T(8,128)(2,1)S(1)} %convert.75), channel_id=1, source_target_pairs={{0,9},{1,10},{2,11},{3,12},{4,13},{5,14},{6,15},{7,16},{8,17},{9,1... | collective-permute-start | bytes 24584
  342.2 16.6 %collective-permute-start.31 = (bf16[16,256]{1,0:T(8,128)(2,1)S(1)}, bf16[16,256]{1,0:T(8,128)(2,1)S(1)}, u32[]{:S(2)}, u32[]{:S(2)}) collective-permute-start(bf16[16,256]{1,0:T(8,128)(2,1)S(1)} %convert.75), channel_id=1, source_target_pairs={{0,8},{1,9},{2,10},{3,11},{4,12},{5,13},{6,14},{7,15},{8,16},{9,17... | collective-permute-start | bytes 24584
  345.5 15.5 %collective-permute-start.30 = (bf16[16,256]{1,0:T(8,128)(2,1)S(1)}, bf16[16,256]{1,0:T(8,128)(2,1)S(1)}, u32[]{:S(2)}, u32[]{:S(2)}) collective-permute-start(bf16[16,256]{1,0:T(8,128)(2,1)S(1)} %convert.75), channel_id=1, source_target_pairs={{0,7},{1,8},{2,9},{3,10},{4,11},{5,12},{6,13},{7,14},{8,15},{9,16}... | collective-permute-start | bytes 24584
  348.2 15.0 %collective-permute-start.29 = (bf16[16,256]{1,0:T(8,128)(2,1)S(1)}, bf16[16,256]{1,0:T(8,128)(2,1)S(1)}, u32[]{:S(2)}, u32[]{:S(2)}) collective-permute-start(bf16[16,256]{1,0:T(8,128)(2,1)S(1)} %convert.75), channel_id=1, source_target_pairs={{0,6},{1,7},{2,8},{3,9},{4,10},{5,11},{6,12},{7,13},{8,14},{9,15},... | collective-permute-start | bytes 24584
  352.4 13.0 %collective-permute-start.28 = (bf16[16,256]{1,0:T(8,128)(2,1)S(1)}, bf16[16,256]{1,0:T(8,128)(2,1)S(1)}, u32[]{:S(2)}, u32[]{:S(2)}) collective-permute-start(bf16[16,256]{1,0:T(8,128)(2,1)S(1)} %convert.75), channel_id=1, source_target_pairs={{0,5},{1,6},{2,7},{3,8},{4,9},{5,10},{6,11},{7,12},{8,13},{9,14},{... | collective-permute-start | bytes 24584
  354.3 12.9 %collective-permute-start.27 = (bf16[16,256]{1,0:T(8,128)(2,1)S(1)}, bf16[16,256]{1,0:T(8,128)(2,1)S(1)}, u32[]{:S(2)}, u32[]{:S(2)}) collective-permute-start(bf16[16,256]{1,0:T(8,128)(2,1)S(1)} %convert.75), channel_id=1, source_target_pairs={{0,4},{1,5},{2,6},{3,7},{4,8},{5,9},{6,10},{7,11},{8,12},{9,13},{1... | collective-permute-start | bytes 24584
  358.8 14.6 %collective-permute-start.26 = (bf16[16,256]{1,0:T(8,128)(2,1)S(1)}, bf16[16,256]{1,0:T(8,128)(2,1)S(1)}, u32[]{:S(2)}, u32[]{:S(2)}) collective-permute-start(bf16[16,256]{1,0:T(8,128)(2,1)S(1)} %convert.75), channel_id=1, source_target_pairs={{0,3},{1,4},{2,5},{3,6},{4,7},{5,8},{6,9},{7,10},{8,11},{9,12},{10... | collective-permute-start | bytes 24584
  361.0 14.9 %collective-permute-start.25 = (bf16[16,256]{1,0:T(8,128)(2,1)S(1)}, bf16[16,256]{1,0:T(8,128)(2,1)S(1)}, u32[]{:S(2)}, u32[]{:S(2)}) collective-permute-start(bf16[16,256]{1,0:T(8,128)(2,1)S(1)} %convert.75), channel_id=1, source_target_pairs={{0,2},{1,3},{2,4},{3,5},{4,6},{5,7},{6,8},{7,9},{8,10},{9,11},{10,... | collective-permute-start | bytes 24584
  363.2 14.6 %collective-permute-start.24 = (bf16[16,256]{1,0:T(8,128)(2,1)S(1)}, bf16[16,256]{1,0:T(8,128)(2,1)S(1)}, u32[]{:S(2)}, u32[]{:S(2)}) collective-permute-start(bf16[16,256]{1,0:T(8,128)(2,1)S(1)} %convert.75), channel_id=1, source_target_pairs={{0,1},{1,2},{2,3},{3,4},{4,5},{5,6},{6,7},{7,8},{8,9},{9,10},{10,1... | collective-permute-start | bytes 24584
  365.4 16.8 %collective-permute-start.46 = (bf16[12,256]{1,0:T(8,128)(2,1)S(1)}, bf16[12,256]{1,0:T(8,128)(2,1)S(1)}, u32[]{:S(2)}, u32[]{:S(2)}) collective-permute-start(bf16[12,256]{1,0:T(8,128)(2,1)S(1)} %slice.609), channel_id=1, source_target_pairs={{0,7},{1,8},{2,9},{3,10},{4,11},{5,12},{6,13},{7,14},{8,15},{9,16}... | collective-permute-start | bytes 18440
  367.2 17.0 %collective-permute-start.45 = (bf16[40,256]{1,0:T(8,128)(2,1)S(1)}, bf16[40,256]{1,0:T(8,128)(2,1)S(1)}, u32[]{:S(2)}, u32[]{:S(2)}) collective-permute-start(bf16[40,256]{1,0:T(8,128)(2,1)S(1)} %convert.74), channel_id=1, source_target_pairs={{0,6},{1,7},{2,8},{3,9},{4,10},{5,11},{6,12},{7,13},{8,14},{9,15},... | collective-permute-start | bytes 61448
  373.4 14.1 %collective-permute-start.44 = (bf16[40,256]{1,0:T(8,128)(2,1)S(1)}, bf16[40,256]{1,0:T(8,128)(2,1)S(1)}, u32[]{:S(2)}, u32[]{:S(2)}) collective-permute-start(bf16[40,256]{1,0:T(8,128)(2,1)S(1)} %convert.74), channel_id=1, source_target_pairs={{0,5},{1,6},{2,7},{3,8},{4,9},{5,10},{6,11},{7,12},{8,13},{9,14},{... | collective-permute-start | bytes 61448
  375.9 11.6 %collective-permute-start.43 = (bf16[40,256]{1,0:T(8,128)(2,1)S(1)}, bf16[40,256]{1,0:T(8,128)(2,1)S(1)}, u32[]{:S(2)}, u32[]{:S(2)}) collective-permute-start(bf16[40,256]{1,0:T(8,128)(2,1)S(1)} %convert.74), channel_id=1, source_target_pairs={{0,4},{1,5},{2,6},{3,7},{4,8},{5,9},{6,10},{7,11},{8,12},{9,13},{1... | collective-permute-start | bytes 61448
  377.9 9.7 %collective-permute-start.42 = (bf16[40,256]{1,0:T(8,128)(2,1)S(1)}, bf16[40,256]{1,0:T(8,128)(2,1)S(1)}, u32[]{:S(2)}, u32[]{:S(2)}) collective-permute-start(bf16[40,256]{1,0:T(8,128)(2,1)S(1)} %convert.74), channel_id=1, source_target_pairs={{0,3},{1,4},{2,5},{3,6},{4,7},{5,8},{6,9},{7,10},{8,11},{9,12},{10... | collective-permute-start | bytes 61448
  387.5 78.7 %reduce-scatter.13.cloned.1.call-start = ((), (), s32[]{:S(2)}) async-start(), calls=%async_computation.3 | async-start | bytes 73728
  (34 other events, 288.3 us)
Sparse Core Ops, SparseCore 0:
  387.6 32.2 reduce-scatter.10
  422.9 43.1 reduce-scatter.12
where the time goes:
time: 480 us; the launch traced here: 474 us
  starting transfers between devices  183 us (38%)
  blocking collectives  151 us (31%)
  waiting for transfers between devices  84.2 us (18%)
  local copies, waits for them, and re-layouts  20.3 us (4%)
  between operations  16.3 us (3%)
  matrix products  12 us (2%)
  other arithmetic  7.66 us (2%)
    unnamed x1, blocking collectives  151 us
    unnamed x25, starting transfers between devices  101 us
    unnamed x27, waiting for transfers between devices  73.8 us
    ppermute x12, starting transfers between devices, extended(): lax.ppermute(tail, axis, [(i, (i + 1) % count) for i in range(ends)])  54.9 us
    ppermute x12, starting transfers between devices, extended(): lax.ppermute(head, axis, [((i + 1) % count, i) for i in range(ends)])  27.7 us
  transfers between devices with their start and end apart: 49, of which 13 were waited for; matrix products, arithmetic and copies ran while one was open for 4% of the time, Pallas kernels for 0%

commit v1 on v0

v1 whole, which is shorter than its diff:
```python
import functools
from types import SimpleNamespace

import jax
import jax.numpy as jnp
import ml_dtypes
import numpy as np
from jax import lax
from jax.experimental import pallas as pl
from jax.experimental.pallas import tpu as pltpu
from jax.sharding import PartitionSpec as P

BF = jnp.bfloat16
F32 = jnp.float32
MESH = pl.DeviceIdType.MESH
C = 256
NR, NC = 8, 64
LANE = 128


def place(h, w, i, j):
    if j < 0:
        return w * (h + 2) + i + 1
    if j >= w:
        return w * (h + 2) + 16 + i + 1
    return (i + 1) * w + j


def size(h, w):
    return w * (h + 2) + 32


def cells(h, w):
    return [(i, j) for i in range(-1, h + 1) for j in range(-1, w + 1)]


def clamp(i, n, kind):
    if kind == 1:
        i = max(i, 0)
    if kind == 2:
        i = min(i, n - 1)
    return i


def up_taps(i):
    k = i // 2
    if i % 2 == 0:
        return [(k - 1, 0.25), (k, 0.75)]
    return [(k, 0.75), (k + 1, 0.25)]


def up_matrix(h, w, pad):
    mat = np.zeros((9, size(2 * h, 2 * w), pad), np.float32)
    for v in range(9):
        for i, j in cells(2 * h, 2 * w):
            for ri, rw in up_taps(i):
                for ci, cw in up_taps(j):
                    ri2, ci2 = clamp(ri, h, v // 3), clamp(ci, w, v % 3)
                    mat[v, place(2 * h, 2 * w, i, j), place(h, w, ri2, ci2)] += rw * cw
    return mat.astype(ml_dtypes.bfloat16)


def down_matrix(h, w, rows, pad):
    mat = np.zeros((9, rows, pad), np.float32)
    weights = (0.25, 0.75, 0.75, 0.25)
    for v in range(9):
        for i in range(h):
            for j in range(w):
                for a in range(4):
                    for b in range(4):
                        ri = clamp(2 * i - 1 + a, 2 * h, v // 3)
                        ci = clamp(2 * j - 1 + b, 2 * w, v % 3)
                        mat[v, i * w + j, place(2 * h, 2 * w, ri, ci)] += weights[a] * weights[b]
    return mat.astype(ml_dtypes.bfloat16)


def pack_matrix(h, w, first, cols):
    mat = np.zeros((32, cols), np.float32)
    for i in range(h):
        mat[first + i, i * w] = 1
        mat[16 + first + i, i * w + w - 1] = 1
    return mat.astype(ml_dtypes.bfloat16)


def side_matrix(levels):
    mat = np.zeros((32 * len(levels), LANE), np.float32)
    for n, (h, first) in enumerate(levels):
        for side in range(2):
            row, src = 32 * n + 16 * side, 48 * side
            mat[row, src + 16 + first + h - 1] = 1
            for i in range(h):
                mat[row + 1 + i, src + first + i] = 1
            mat[row + 1 + h, src + 32 + first] = 1
    return mat.astype(ml_dtypes.bfloat16)


def constants():
    packs = [
        pack_matrix(8, 64, 0, 512),
        pack_matrix(4, 32, 8, 128),
        pack_matrix(2, 16, 12, 32),
        pack_matrix(4, 32, 0, 128),
    ]
    return dict(
        u1=up_matrix(2, 16, 128),
        u2=up_matrix(4, 32, 256),
        d1=down_matrix(4, 32, 128, 768),
        d2=down_matrix(2, 16, 128, 256),
        pf=packs[0],
        pm=packs[1],
        pc=np.concatenate([packs[2], np.zeros((32, 96), ml_dtypes.bfloat16)], 1),
        pm0=packs[3],
        s1=side_matrix([(8, 0), (4, 8), (2, 12)]),
        sf=side_matrix([(8, 0)]),
        sm=side_matrix([(4, 0)]),
    )


CP, CQ, LP, LQ = 640, 512, 128, 256


def dot(a, b):
    return jnp.dot(a, b, preferred_element_type=F32)


def dot_t(a, b):
    return lax.dot_general(a, b, (((1,), (1,)), ((), ())), preferred_element_type=F32)


def kernel(consts, *refs):
    fin, mid, coa, wl, wo_hbm, cot = refs[:6]
    k = SimpleNamespace(**dict(zip(consts, refs[6 : 6 + len(consts)])))
    o_mask, o_fine, o_mid, o_coa, o_lat, o_conv = refs[6 + len(consts) : 12 + len(consts)]
    g = SimpleNamespace(**dict(zip(SCRATCH, refs[12 + len(consts) :])))
    r, c = lax.axis_index("rows"), lax.axis_index("cols")
    y, x_lo = r // 2, r % 2
    x_hi, z, core = c // 32, (c // 2) % 16, c % 2
    x = x_hi * 2 + x_lo
    z_hi, z_lo = z // 4, z % 4
    other = 1 - core
    e_n, e_s = 1 - (r + NR - 1) // NR, (r + 1) // NR
    e_w, e_e = 1 - (c + NC - 1) // NC, (c + 1) // NC
    variant = (e_n + 2 * e_s) * 3 + e_w + 2 * e_e

    up, down = (r + NR - 1) % NR, (r + 1) % NR
    left, right = (c + NC - 1) % NC, (c + 1) % NC

    def dev_x(d):
        t = (x + d) % 4
        return (y * 2 + t % 2, (t // 2) * 32 + z * 2 + core), t

    def dev_y(d):
        t = (y + d) % 4
        return (t * 2 + x_lo, c), t

    def dev_zlo(d):
        t = (z_lo + d) % 4
        return (r, x_hi * 32 + (z_hi * 4 + t) * 2 + core), t

    def dev_zhi(d, k):
        t = (z_hi + d) % 4
        return (r, x_hi * 32 + (t * 4 + z_lo) * 2 + k), t

    partner = (r, x_hi * 32 + z * 2 + other)

    loads = []

    def load(src, dst):
        copy = pltpu.make_async_copy(src, dst, g.lsem.at[len(loads)])
        copy.start()
        loads.append(copy)
        return copy

    inputs = [
        load(fin, g.finx.at[64:576]),
        load(mid, g.midx.at[32:160]),
        load(coa, g.coax.at[16:48]),
        load(coa, g.coab.at[0:32]),
        load(k.pf, g.v_pf),
        load(k.pm, g.v_pm),
        load(k.pc, g.v_pc),
    ]
    forward = [
        load(k.s1, g.v_s1),
        load(wl, g.v_wl),
        load(k.u1.at[variant], g.v_u1),
        load(k.u2.at[variant], g.v_u2),
    ]
    load_wo = load(wo_hbm, g.v_wo)
    load_cot = load(cot, g.v_cot)
    load_sf = load(k.sf, g.v_sf)
    backward = [
        load(k.d1.at[variant], g.v_d1),
        load(k.d2.at[variant], g.v_d2),
        load(k.pm0, g.v_pm0),
        load(k.sm, g.v_sm),
    ]

    def wait(copies):
        for copy in copies:
            copy.wait()

    peers = [(up, c), (down, c)] + [(a, b) for a in (r, up, down) for b in (left, right)]
    peers += [partner]
    for d in (1, 2, 3):
        peers += [dev_x(d)[0], dev_y(d)[0], dev_zlo(d)[0], dev_zhi(d, core)[0], dev_zhi(d, other)[0]]
    barrier = pltpu.get_barrier_semaphore()
    for p in peers:
        pl.semaphore_signal(barrier, inc=1, device_id=p, device_id_type=MESH)

    for ref, at, count in ((g.coab, 32, 96), (g.topb, 96, 32), (g.midb, 224, 32), (g.dfx, 672, 96), (g.dmx, 224, 32)):
        ref[at : at + count] = jnp.zeros((count, C), BF)
    for ref in (g.rs1, g.rs2, g.rs3, g.rs4):
        ref[96:128] = jnp.zeros((32, C), BF)

    used = [0]

    def send(src, dst, to):
        n = used[0]
        used[0] += 1
        copy = pltpu.make_async_remote_copy(
            src_ref=src,
            dst_ref=dst,
            send_sem=g.ssem.at[n],
            recv_sem=g.rsem.at[n],
            device_id=to,
            device_id_type=MESH,
        )
        copy.start()
        return copy

    sent = []

    def received(copies):
        for copy in copies:
            copy.wait_recv()
        sent.extend(copies)

    def send_rows(buf, h, w):
        return [
            send(buf.at[w : 2 * w], buf.at[w * (h + 1) : w * (h + 2)], (up, c)),
            send(buf.at[w * h : w * (h + 1)], buf.at[0:w], (down, c)),
        ]

    def send_sides(pack, slots):
        west, east = pack.at[0:16], pack.at[16:32]

        def slot(n):
            return slots.at[16 * n : 16 * n + 16]

        return [
            send(east, slot(0), (r, right)),
            send(east, slot(1), (down, right)),
            send(east, slot(2), (up, right)),
            send(west, slot(3), (r, left)),
            send(west, slot(4), (down, left)),
            send(west, slot(5), (up, left)),
        ]

    wait(inputs)
    packed = dot(g.v_pf[...], g.finx[64:576])
    packed += dot(g.v_pm[...], g.midx[32:160])
    packed += dot(g.v_pc[...], g.coab[...])
    g.pk1[...] = packed.astype(BF)
    pl.semaphore_wait(barrier, len(peers))
    halo = send_sides(g.pk1, g.rs1)
    halo += send_rows(g.coax, 2, 16)
    halo += send_rows(g.midx, 4, 32)
    halo += send_rows(g.finx, 8, 64)
    wait(forward)
    received(halo)
    sides = dot(g.v_s1[...], g.rs1[...]).astype(BF)
    g.finx[640:672] = sides[0:32]
    g.midx[192:224] = sides[32:64]
    g.coax[64:96] = sides[64:96]

    wl = g.v_wl
    w_fine, w_mid, w_top = wl[0:C], wl[C : 2 * C], wl[2 * C : 3 * C]
    g.topb[0:96] = dot(g.coax[0:96], w_top).astype(BF)
    g.midb[0:224] = (dot(g.midx[...], w_mid) + dot(g.v_u1[...], g.topb[...])).astype(BF)
    g.fex[...] = dot(g.finx[...], w_fine) + dot(g.v_u2[...], g.midb[...])

    keep_n, keep_s = (1 - e_n).astype(F32), (1 - e_s).astype(F32)
    keep_w, keep_e = (1 - e_w).astype(F32), (1 - e_e).astype(F32)
    line = lax.broadcasted_iota(jnp.int32, (16, C), 0)
    keep_rows = jnp.where(line == 0, keep_n, jnp.where(line == 9, keep_s, 1.0))

    def spread(north, body, south, west, east, out, flip):
        s = g.shift
        s[0, 8:72] = north * keep_n
        s[1:9, 8:72] = body.reshape(8, 64, C)
        s[9, 8:72] = south * keep_s
        west = west * (keep_rows * keep_w)
        east = east * (keep_rows * keep_e)
        for i in range(10):
            s[i, 7:8] = west[i : i + 1]
            s[i, 72:73] = east[i : i + 1]
        for b in range(3):
            at = 9 - b if flip else 7 + b
            out[:, b * C : (b + 1) * C] = s[:, at : at + 64].astype(BF).reshape(640, C)

    fex = g.fex
    spread(fex[0:64], fex[64:576], fex[576:640], fex[640:656], fex[656:672], g.fsh, False)

    load_wo.wait()
    wo, fsh, dsh = g.v_wo, g.fsh, g.dsh
    g.pre[...] = sum(dot(fsh[64 * a : 64 * a + 512], wo[768 * a : 768 * a + 768]) for a in range(3))
    load_cot.wait()

    def activate(q, carry):
        at = pl.multiple_of(q * 64, 64)
        v = g.pre[pl.ds(at, 64)]
        half = 0.5 + 0.5 * lax.erf(v * np.float32(np.sqrt(0.5)))
        g.maskb[pl.ds(at, 64)] = (v * half).astype(BF)
        slope = half + v * (jnp.exp(-0.5 * v * v) * np.float32(1 / np.sqrt(2 * np.pi)))
        g.dpx[pl.ds(at + 64, 64)] = (g.v_cot[pl.ds(at, 64)].astype(F32) * slope).astype(BF)
        return carry

    lax.fori_loop(0, 8, activate, 0)
    stores = []

    def store(src, dst):
        copy = pltpu.make_async_copy(src, dst, g.osem.at[len(stores)])
        copy.start()
        stores.append(copy)

    store(g.maskb, o_mask)

    load_sf.wait()
    halo = send_rows(g.dpx, 8, 64)
    g.pk2[...] = dot(g.v_pf[...], g.dpx[64:576]).astype(BF)
    halo += send_sides(g.pk2, g.rs2)

    grad, got = g.grad, g.got
    dpre_t = g.dpx[64:576].T
    pair = []
    for a in range(3):
        lanes = pl.ds(768 * a, 768)
        term = dot(dpre_t, fsh[64 * a : 64 * a + 512]).astype(BF)
        grad[:, :, :, lanes] = term.reshape(8, 2, 16, 768)
        pair.append(send(grad.at[:, other, :, lanes], got.at[:, :, lanes], partner))

    received(halo)
    sides = dot(g.v_sf[...], g.rs2[...])
    dpx = g.dpx
    spread(
        dpx[0:64].astype(F32), dpx[64:576].astype(F32), dpx[576:640].astype(F32),
        sides[0:16], sides[16:32], dsh, True,
    )
    dfine = None
    for a in range(3):
        for b in range(3):
            t = 3 * a + b
            term = dot_t(dsh[64 * (2 - a) : 64 * (2 - a) + 512, b * C : (b + 1) * C], wo[t * C : (t + 1) * C])
            dfine = term if dfine is None else dfine + term
    dfx = g.dfx
    dfx[64:576] = dfine.astype(BF)
    halo = send_rows(dfx, 8, 64)
    g.pk3[...] = dot(g.v_pf[...], dfx[64:576]).astype(BF)
    halo += send_sides(g.pk3, g.rs3)

    def begin(buf, slots, dev):
        out = []
        for d in (1, 2, 3):
            to, t = dev(d)
            out.append(send(buf.at[t], slots.at[d - 1], to))
        return out

    def total(buf, mine, slots):
        return buf[mine].astype(F32) + slots[0].astype(F32) + slots[1].astype(F32) + slots[2].astype(F32)

    def split(mine, theirs, half, first, p, q):
        wp, wq = p.shape[-1], q.shape[-1]
        for n in range(8):
            part = (mine[n, core].astype(F32) + theirs[n].astype(F32)).astype(BF)
            for h in range(2):
                at = half * h
                p[2 * h + n % 2, n // 2] = part[:, at : at + wp]
                q[n // 2, 2 * h + n % 2] = part[:, at + wp : at + wp + wq]

    received(pair)
    split(grad, got, 1152, 0, g.cp1, g.cq1)
    cp = begin(g.cp1, g.cp1r, dev_x)
    cq = begin(g.cq1, g.cq1r, dev_y)

    g.fgb[...] = dot_t(dfx[64:576], w_fine).astype(BF)
    store(g.fgb, o_fine)
    lgrad, lgot = g.lgrad, g.lgot
    lgrad[:, :, :, 0:C] = dot(dfx[64:576].T, g.finx[64:576]).astype(BF).reshape(8, 2, 16, C)
    lpair = [send(lgrad.at[:, other, :, pl.ds(0, C)], lgot.at[:, :, pl.ds(0, C)], partner)]

    received(halo)
    wait(backward)
    dfx[640:672] = dot(g.v_sf[...], g.rs3[...]).astype(BF)
    dmx = g.dmx
    dmx[32:160] = dot(g.v_d1[...], dfx[...]).astype(BF)
    halo = send_rows(dmx, 4, 32)
    g.pk4[...] = dot(g.v_pm0[...], dmx[32:160]).astype(BF)
    halo += send_sides(g.pk4, g.rs4)

    received(cp)
    g.cp2[...] = total(g.cp1, x, g.cp1r).astype(BF)
    cp = begin(g.cp2, g.cp2r, dev_y)
    received(cq)
    g.cq2[...] = total(g.cq1, y, g.cq1r).astype(BF)
    cq = begin(g.cq2, g.cq2r, dev_x)

    g.mgb[...] = dot_t(dmx[32:160], w_mid).astype(BF)
    store(g.mgb, o_mid)
    lgrad[:, :, :, C : 2 * C] = dot(dmx[32:160].T, g.midx[32:160]).astype(BF).reshape(8, 2, 16, C)
    lpair += [send(lgrad.at[:, other, :, pl.ds(C, C)], lgot.at[:, :, pl.ds(C, C)], partner)]

    received(halo)
    dmx[192:224] = dot(g.v_sm[...], g.rs4[...]).astype(BF)
    dtop = dot(g.v_d2[...], dmx[...]).astype(BF)
    g.cgb[...] = dot_t(dtop[0:32], w_top).astype(BF)
    store(g.cgb, o_coa)
    lgrad[:, :, :, 2 * C : 3 * C] = dot(dtop.T, g.coab[...]).astype(BF).reshape(8, 2, 16, C)
    lpair += [send(lgrad.at[:, other, :, pl.ds(2 * C, C)], lgot.at[:, :, pl.ds(2 * C, C)], partner)]

    received(lpair)
    split(lgrad, lgot, 384, 0, g.lp1, g.lq1)
    lp = begin(g.lp1, g.lp1r, dev_x)
    lq = begin(g.lq1, g.lq1r, dev_y)
    sums = g.sums
    received(cp)
    sums[:, 0:CP] = total(g.cp2, y, g.cp2r)
    received(cq)
    sums[:, CP : CP + CQ] = total(g.cq2, x, g.cq2r)
    received(lp)
    g.lp2[...] = total(g.lp1, x, g.lp1r).astype(BF)
    lp = begin(g.lp2, g.lp2r, dev_y)
    received(lq)
    g.lq2[...] = total(g.lq1, y, g.lq1r).astype(BF)
    lq = begin(g.lq2, g.lq2r, dev_x)
    received(lp)
    sums[:, 1152 : 1152 + LP] = total(g.lp2, y, g.lp2r)
    received(lq)
    sums[:, 1152 + LP : 1536] = total(g.lq2, x, g.lq2r)

    lane = lax.broadcasted_iota(jnp.int32, (16, LANE), 1)

    def window(base, count, start):
        t, off = start // LANE, start % LANE

        def tile(n):
            n = min(max(n, 0), count // LANE - 1)
            return sums[:, base + n * LANE : base + (n + 1) * LANE]

        if off == 0:
            return tile(t)
        return jnp.where(
            lane < LANE - off,
            pltpu.roll(tile(t), LANE - off, 1),
            pltpu.roll(tile(t + 1), LANE - off, 1),
        )

    for n in range(16):
        conv = window(0, 1152, 72 * n)
        lat = window(1152, 384, 24 * n - 72)
        g.z1[n % 4, n // 4] = jnp.where(lane < 72, conv, lat).astype(BF)
    zc = begin(g.z1, g.z1r, dev_zlo)
    received(zc)
    g.z2[...] = total(g.z1, z_lo, g.z1r).astype(BF)
    z2, fin = g.z2, g.fin_r
    zc = [send(z2.at[z_hi], fin.at[1, 0], partner)]
    for d in (1, 2, 3):
        for e, k in ((0, core), (1, other)):
            to, t = dev_zhi(d, k)
            zc.append(send(z2.at[t], fin.at[e, d], to))
    received(zc)
    same = z2[z_hi].astype(F32) + sum(fin[0, d].astype(F32) for d in (1, 2, 3))
    cross = sum(fin[1, d].astype(F32) for d in range(4))
    first = core == 0
    rows32 = [jnp.where(first, same, cross), jnp.where(first, cross, same)]
    g.turn[...] = jnp.concatenate(rows32 + [jnp.zeros((96, LANE), F32)], 0).T
    turn = g.turn
    o_conv[...] = jnp.where(first, turn[0:36, 0:32], turn[36:72, 0:32])
    o_lat[...] = jnp.where(first, turn[72:84, 0:32], turn[84:96, 0:32])

    for copy in sent:
        copy.wait_send()
    wait(stores)


VM = pltpu.VMEM
DMA = pltpu.SemaphoreType.DMA
SCRATCH = dict(
    finx=VM((672, C), BF),
    midx=VM((224, C), BF),
    coax=VM((96, C), BF),
    coab=VM((128, C), BF),
    v_wl=VM((768, C), BF),
    v_wo=VM((2304, C), BF),
    v_cot=VM((512, C), BF),
    v_u1=VM((224, 128), BF),
    v_u2=VM((672, 256), BF),
    v_d1=VM((128, 768), BF),
    v_d2=VM((128, 256), BF),
    v_pf=VM((32, 512), BF),
    v_pm=VM((32, 128), BF),
    v_pc=VM((32, 128), BF),
    v_pm0=VM((32, 128), BF),
    v_s1=VM((96, 128), BF),
    v_sf=VM((32, 128), BF),
    v_sm=VM((32, 128), BF),
    topb=VM((128, C), BF),
    midb=VM((256, C), BF),
    fex=VM((672, C), F32),
    shift=VM((10, 80, C), F32),
    fsh=VM((640, 768), BF),
    dsh=VM((640, 768), BF),
    pre=VM((512, C), F32),
    maskb=VM((512, C), BF),
    dpx=VM((640, C), BF),
    dfx=VM((768, C), BF),
    dmx=VM((256, C), BF),
    fgb=VM((512, C), BF),
    mgb=VM((128, C), BF),
    cgb=VM((32, C), BF),
    pk1=VM((32, C), BF),
    pk2=VM((32, C), BF),
    pk3=VM((32, C), BF),
    pk4=VM((32, C), BF),
    rs1=VM((128, C), BF),
    rs2=VM((128, C), BF),
    rs3=VM((128, C), BF),
    rs4=VM((128, C), BF),
    grad=VM((8, 2, 16, 2304), BF),
    got=VM((8, 16, 2304), BF),
    lgrad=VM((8, 2, 16, 768), BF),
    lgot=VM((8, 16, 768), BF),
    cp1=VM((4, 4, 16, CP), BF),
    cp1r=VM((3, 4, 16, CP), BF),
    cp2=VM((4, 16, CP), BF),
    cp2r=VM((3, 16, CP), BF),
    cq1=VM((4, 4, 16, CQ), BF),
    cq1r=VM((3, 4, 16, CQ), BF),
    cq2=VM((4, 16, CQ), BF),
    cq2r=VM((3, 16, CQ), BF),
    lp1=VM((4, 4, 16, LP), BF),
    lp1r=VM((3, 4, 16, LP), BF),
    lp2=VM((4, 16, LP), BF),
    lp2r=VM((3, 16, LP), BF),
    lq1=VM((4, 4, 16, LQ), BF),
    lq1r=VM((3, 4, 16, LQ), BF),
    lq2=VM((4, 16, LQ), BF),
    lq2r=VM((3, 16, LQ), BF),
    sums=VM((16, 1536), F32),
    z1=VM((4, 4, 16, LANE), BF),
    z1r=VM((3, 4, 16, LANE), BF),
    z2=VM((4, 16, LANE), BF),
    fin_r=VM((2, 4, 16, LANE), BF),
    turn=VM((128, 128), F32),
    lsem=DMA((20,)),
    osem=DMA((4,)),
    ssem=DMA((80,)),
    rsem=DMA((80,)),
)


def local(consts, fine_in, mid_in, coarse_in, lateral_weight, out_weight, cotangent):
    def flat(v):
        return v.reshape(-1, v.shape[-1])

    args = [flat(fine_in), flat(mid_in), flat(coarse_in), lateral_weight, out_weight, flat(cotangent)]
    args += [jnp.asarray(v) for v in consts.values()]
    hbm = pl.BlockSpec(memory_space=pl.ANY)
    vmem = pl.BlockSpec(memory_space=pltpu.VMEM)
    outs = pl.pallas_call(
        functools.partial(kernel, tuple(consts)),
        out_shape=[
            jax.ShapeDtypeStruct((512, C), BF),
            jax.ShapeDtypeStruct((512, C), BF),
            jax.ShapeDtypeStruct((128, C), BF),
            jax.ShapeDtypeStruct((32, C), BF),
            jax.ShapeDtypeStruct((12, 32), F32),
            jax.ShapeDtypeStruct((36, 32), F32),
        ],
        in_specs=[hbm] * len(args),
        out_specs=[hbm] * 4 + [vmem] * 2,
        scratch_shapes=list(SCRATCH.values()),
        compiler_params=pltpu.CompilerParams(
            collective_id=0, has_side_effects=True, vmem_limit_bytes=40 * 2**20
        ),
        cost_estimate=pl.CostEstimate(flops=2_400_000_000, bytes_accessed=4_000_000, transcendentals=262144),
    )(*args)
    return (
        outs[0].reshape(fine_in.shape),
        outs[1].reshape(fine_in.shape),
        outs[2].reshape(mid_in.shape),
        outs[3].reshape(coarse_in.shape),
        outs[4],
        outs[5],
    )


def solution(mesh):
    field = P("rows", "cols", None)
    return jax.shard_map(
        functools.partial(local, constants()),
        mesh=mesh,
        in_specs=(field, field, field, P(), P(), field),
        out_specs=(field, field, field, field, P("cols", "rows"), P("cols", "rows")),
        check_vma=False,
    )
```

time: 480 us -> 86 us (0.18)
  starting transfers between devices: 183 us -> 0 us
  blocking collectives: 151 us -> 0 us
  waiting for transfers between devices: 84.2 us -> 0 us
  Pallas kernels: 0 us -> 64.4 us
  between operations: 16.3 us -> 0.67 us
  matrix products: 12 us -> 0 us
  other arithmetic: 7.66 us -> 0 us
    unnamed x1 -> x0, blocking collectives: 151 us -> none
    unnamed x25 -> x0, starting transfers between devices: 101 us -> none
    ppermute x24 -> x0, starting transfers between devices: 82.6 us -> none  [the longest x12 54.9 us: extended(): lax.ppermute(tail, axis, [(i, (i + 1) % count) for i in range(ends)])]
    unnamed x27 -> x0, waiting for transfers between devices: 73.8 us -> none
    pallas_call x0 -> x1, Pallas kernels: none -> 64.4 us  [local(): pl.pallas_call(functools.partial(kernel, tuple(consts)), out_shape=[jax.S...]
    dot_general x12 -> x0, matrix products: 12 us -> none  [the longest x6 6.88 us: lateral(): jnp.dot(feature.reshape(height * width, chans), weight, preferred_element...]
    unnamed x43 -> x40, local copies, waits for them, and re-layouts: 9.3 us -> 20.1 us
    ppermute x24 -> x0, waiting for transfers between devices: 10.4 us -> none  [the longest x12 7.32 us: extended(): lax.ppermute(tail, axis, [(i, (i + 1) % count) for i in range(ends)])]
  transfers between devices with their start and end apart: 49 -> 0, of which waited for: 13 -> 0; matrix products, arithmetic and copies ran while one was open for 4% -> 0% of each run, Pallas kernels for 0% -> 0%
where the time goes in v1:
time: 86 us; the launch traced here: 85.1 us
  Pallas kernels  64.4 us (75%)
  local copies, waits for them, and re-layouts  20.1 us (23%)
    pallas_call x1, Pallas kernels, local(): pl.pallas_call(functools.partial(kernel, tuple(consts)), out_shape=[jax.S...  64.4 us
    unnamed x40, local copies, waits for them, and re-layouts  20.1 us

profile of v1, /device:TPU:1, one launch (start us, length us, event | category | flops | bytes accessed | tf_op | source)
XLA Modules:
  0.0 85.1 jit_solution(11941198455350994172)
XLA Ops:
  0.6 1.3 %copy-done = bf16[2304,256]{1,0:T(8,128)(2,1)S(1)} copy-done((bf16[2304,256]{1,0:T(8,128)(2,1)S(1)}, bf16[2304,256]{1,0:T(8,128)(2,1)}, u32[]{:S(2)}) %copy-start) | copy-done | bytes 1179672
  1.9 1.0 %copy-done.1 = bf16[768,256]{1,0:T(8,128)(2,1)S(1)} copy-done((bf16[768,256]{1,0:T(8,128)(2,1)S(1)}, bf16[768,256]{1,0:T(8,128)(2,1)}, u32[]{:S(2)}) %copy-start.1) | copy-done | bytes 393240
  2.9 0.9 %copy-done.2 = bf16[8,64,256]{2,1,0:T(8,128)(2,1)S(1)} copy-done((bf16[8,64,256]{2,1,0:T(8,128)(2,1)S(1)}, bf16[8,64,256]{2,1,0:T(8,128)(2,1)}, u32[]{:S(2)}) %copy-start.2) | copy-done | bytes 262168
  3.9 0.9 %copy-done.3 = bf16[8,64,256]{2,1,0:T(8,128)(2,1)S(1)} copy-done((bf16[8,64,256]{2,1,0:T(8,128)(2,1)S(1)}, bf16[8,64,256]{2,1,0:T(8,128)(2,1)}, u32[]{:S(2)}) %copy-start.3) | copy-done | bytes 262168
  4.8 0.8 copy-done.4
  5.6 0.7 copy-done.5
  6.4 1.9 %copy-done.6 = bf16[9,672,256]{2,1,0:T(8,128)(2,1)S(1)} copy-done((bf16[9,672,256]{2,1,0:T(8,128)(2,1)S(1)}, bf16[9,672,256]{2,1,0:T(8,128)(2,1)}, u32[]{:S(2)}) %copy-start.6) | copy-done | bytes 3096600
  8.2 1.5 %copy-done.7 = bf16[9,128,768]{2,1,0:T(8,128)(2,1)S(1)} copy-done((bf16[9,128,768]{2,1,0:T(8,128)(2,1)S(1)}, bf16[9,128,768]{2,1,0:T(8,128)(2,1)}, u32[]{:S(2)}) %copy-start.7) | copy-done | bytes 1769496
  9.7 1.1 %copy-done.8 = bf16[9,128,256]{2,1,0:T(8,128)(2,1)S(1)} copy-done((bf16[9,128,256]{2,1,0:T(8,128)(2,1)S(1)}, bf16[9,128,256]{2,1,0:T(8,128)(2,1)}, u32[]{:S(2)}) %copy-start.8) | copy-done | bytes 589848
  10.8 1.0 %copy-done.9 = bf16[9,224,128]{2,1,0:T(8,128)(2,1)S(1)} copy-done((bf16[9,224,128]{2,1,0:T(8,128)(2,1)S(1)}, bf16[9,224,128]{2,1,0:T(8,128)(2,1)}, u32[]{:S(2)}) %copy-start.9) | copy-done | bytes 516120
  11.8 0.8 copy-done.10
  12.6 0.7 copy-done.11
  13.3 0.7 copy-done.12
  14.0 0.7 copy-done.13
  14.7 0.7 copy-done.14
  15.4 0.7 copy-done.15
  16.1 0.7 copy-done.16
  16.8 64.4 %shard_map.208 = (bf16[512,256]{1,0:T(8,128)(2,1)S(1)}, bf16[512,256]{1,0:T(8,128)(2,1)S(1)}, bf16[128,256]{1,0:T(8,128)(2,1)S(1)}, bf16[32,256]{1,0:T(8,128)(2,...) custom-call(bf16[512,256]{1,0:T(8,128)(2,1)S(1)} %bitcast.12, bf16[128,256]{1,0:T(8,128)(2,1)S(1)} %bitcast.14, ...), custom_call_target="tpu_custom_call" | custom-call | flops 2400000000 | bytes 4000000 | tf_op jit(solution)/shard_map/pallas_call | solution.py:570
  81.2 0.7 copy.23
  81.9 0.7 copy.29
  82.6 0.7 copy.30
  83.3 0.6 copy.31
  83.9 0.6 copy.32
  84.5 0.6 copy.33
  (17 shorter events, 0.0 us)
Async XLA Ops:
  0.6 1.3 %copy-start = (bf16[2304,256]{1,0:T(8,128)(2,1)S(1)}, bf16[2304,256]{1,0:T(8,128)(2,1)}, u32[]{:S(2)}) copy-start(bf16[2304,256]{1,0:T(8,128)(2,1)} %refs_4_.1) | copy-start | bytes 3538948
  1.9 1.0 %copy-start.1 = (bf16[768,256]{1,0:T(8,128)(2,1)S(1)}, bf16[768,256]{1,0:T(8,128)(2,1)}, u32[]{:S(2)}) copy-start(bf16[768,256]{1,0:T(8,128)(2,1)} %refs_3_.1) | copy-start | bytes 1179652
  2.9 0.9 %copy-start.2 = (bf16[8,64,256]{2,1,0:T(8,128)(2,1)S(1)}, bf16[8,64,256]{2,1,0:T(8,128)(2,1)}, u32[]{:S(2)}) copy-start(bf16[8,64,256]{2,1,0:T(8,128)(2,1)} %param.17) | copy-start | bytes 786436
  3.9 0.9 %copy-start.3 = (bf16[8,64,256]{2,1,0:T(8,128)(2,1)S(1)}, bf16[8,64,256]{2,1,0:T(8,128)(2,1)}, u32[]{:S(2)}) copy-start(bf16[8,64,256]{2,1,0:T(8,128)(2,1)} %param.22) | copy-start | bytes 786436
  4.8 0.8 copy-start.4
  5.6 0.7 copy-start.5
  6.4 1.9 %copy-start.6 = (bf16[9,672,256]{2,1,0:T(8,128)(2,1)S(1)}, bf16[9,672,256]{2,1,0:T(8,128)(2,1)}, u32[]{:S(2)}) copy-start(bf16[9,672,256]{2,1,0:T(8,128)(2,1)} %constant.23.clone.refs_7_) | copy-start | bytes 9289732
  8.2 1.5 %copy-start.7 = (bf16[9,128,768]{2,1,0:T(8,128)(2,1)S(1)}, bf16[9,128,768]{2,1,0:T(8,128)(2,1)}, u32[]{:S(2)}) copy-start(bf16[9,128,768]{2,1,0:T(8,128)(2,1)} %constant.24.clone.refs_8_) | copy-start | bytes 5308420
  9.7 1.1 %copy-start.8 = (bf16[9,128,256]{2,1,0:T(8,128)(2,1)S(1)}, bf16[9,128,256]{2,1,0:T(8,128)(2,1)}, u32[]{:S(2)}) copy-start(bf16[9,128,256]{2,1,0:T(8,128)(2,1)} %constant.25.clone.refs_9_) | copy-start | bytes 1769476
  10.8 1.0 %copy-start.9 = (bf16[9,224,128]{2,1,0:T(8,128)(2,1)S(1)}, bf16[9,224,128]{2,1,0:T(8,128)(2,1)}, u32[]{:S(2)}) copy-start(bf16[9,224,128]{2,1,0:T(8,128)(2,1)} %constant.22.clone.refs_6_) | copy-start | bytes 1548292
  11.8 0.8 copy-start.10
  12.6 0.7 copy-start.11
  13.3 0.7 copy-start.12
  14.0 0.7 copy-start.13
  14.7 0.7 copy-start.14
  15.4 0.7 copy-start.15
  16.1 0.7 copy-start.16

commit v2 on v1

--- a/solution.py
+++ b/solution.py
@@ -74,6 +74,35 @@
     return mat.astype(ml_dtypes.bfloat16)
 
 
+def down_line(n, kind):
+    line = np.zeros((n + 2, 2 * n + 4))
+    for k in range(-1, n + 1):
+        if (kind == 1 and k < 0) or (kind == 2 and k >= n):
+            continue
+        for a, weight in enumerate((0.25, 0.75, 0.75, 0.25)):
+            f = clamp(2 * k - 1 + a, 2 * n, kind)
+            if -2 <= f < 2 * n + 2:
+                line[k + 1, f + 2] += weight
+    return line
+
+
+def adjoint_matrix(h, w, steps, pad):
+    fh, fw = h << steps, w << steps
+    mat = np.zeros((9, fh * fw, pad), np.float32)
+    for v in range(9):
+        lines = []
+        for n, kind in ((h, v // 3), (w, v % 3)):
+            line = down_line(n, kind)
+            for s in range(1, steps):
+                line = line[:, 1:-1] @ down_line(n << s, kind)
+            lines.append(line[:, 2:-2])
+        both = np.multiply.outer(*lines)
+        for i in range(-1, h + 1):
+            for j in range(-1, w + 1):
+                mat[v, :, place(h, w, i, j)] = both[i + 1, :, j + 1, :].reshape(-1)
+    return mat.astype(ml_dtypes.bfloat16)
+
+
 def pack_matrix(h, w, first, cols):
     mat = np.zeros((32, cols), np.float32)
     for i in range(h):
@@ -106,6 +135,8 @@
         u2=up_matrix(4, 32, 256),
         d1=down_matrix(4, 32, 128, 768),
         d2=down_matrix(2, 16, 128, 256),
+        a1=adjoint_matrix(4, 32, 1, 256),
+        a2=adjoint_matrix(2, 16, 2, 128),
         pf=packs[0],
         pm=packs[1],
         pc=np.concatenate([packs[2], np.zeros((32, 96), ml_dtypes.bfloat16)], 1),
@@ -136,7 +167,6 @@
     y, x_lo = r // 2, r % 2
     x_hi, z, core = c // 32, (c // 2) % 16, c % 2
     x = x_hi * 2 + x_lo
-    z_hi, z_lo = z // 4, z % 4
     other = 1 - core
     e_n, e_s = 1 - (r + NR - 1) // NR, (r + 1) // NR
     e_w, e_e = 1 - (c + NC - 1) // NC, (c + 1) // NC
@@ -153,13 +183,9 @@
         t = (y + d) % 4
         return (t * 2 + x_lo, c), t
 
-    def dev_zlo(d):
-        t = (z_lo + d) % 4
-        return (r, x_hi * 32 + (z_hi * 4 + t) * 2 + core), t
-
-    def dev_zhi(d, k):
-        t = (z_hi + d) % 4
-        return (r, x_hi * 32 + (t * 4 + z_lo) * 2 + k), t
+    def dev_z(d):
+        t = (z + d) % 16
+        return (r, x_hi * 32 + t * 2 + core), t
 
     partner = (r, x_hi * 32 + z * 2 + other)
 
@@ -185,6 +211,8 @@
         load(wl, g.v_wl),
         load(k.u1.at[variant], g.v_u1),
         load(k.u2.at[variant], g.v_u2),
+        load(k.a1.at[variant], g.v_a1),
+        load(k.a2.at[variant], g.v_a2),
     ]
     load_wo = load(wo_hbm, g.v_wo)
     load_cot = load(cot, g.v_cot)
@@ -201,14 +229,21 @@
             copy.wait()
 
     peers = [(up, c), (down, c)] + [(a, b) for a in (r, up, down) for b in (left, right)]
-    peers += [partner]
     for d in (1, 2, 3):
-        peers += [dev_x(d)[0], dev_y(d)[0], dev_zlo(d)[0], dev_zhi(d, core)[0], dev_zhi(d, other)[0]]
+        peers += [dev_x(d)[0], dev_y(d)[0]]
+    peers += [dev_z(1)[0], dev_z(15)[0]]
     barrier = pltpu.get_barrier_semaphore()
     for p in peers:
         pl.semaphore_signal(barrier, inc=1, device_id=p, device_id_type=MESH)
 
-    for ref, at, count in ((g.coab, 32, 96), (g.topb, 96, 32), (g.midb, 224, 32), (g.dfx, 672, 96), (g.dmx, 224, 32)):
+    def greet(n):
+        for d in (1 << n, 16 - (1 << n)):
+            pl.semaphore_signal(g.far.at[n], inc=1, device_id=dev_z(d)[0], device_id_type=MESH)
+
+    def met(n):
+        pl.semaphore_wait(g.far.at[n], 2)
+
+    for ref, at, count in ((g.coab, 32, 96), (g.midx, 224, 32), (g.coax, 96, 32), (g.topb, 96, 32), (g.midb, 224, 32), (g.dfx, 672, 96), (g.dmx, 224, 32)):
         ref[at : at + count] = jnp.zeros((count, C), BF)
     for ref in (g.rs1, g.rs2, g.rs3, g.rs4):
         ref[96:128] = jnp.zeros((32, C), BF)
@@ -267,18 +302,25 @@
     halo += send_rows(g.coax, 2, 16)
     halo += send_rows(g.midx, 4, 32)
     halo += send_rows(g.finx, 8, 64)
+    greet(0)
     wait(forward)
+    wl = g.v_wl
+    w_fine, w_mid, w_top = wl[0:C], wl[C : 2 * C], wl[2 * C : 3 * C]
+    fex = g.fex
+    fex[64:576] = dot(g.finx[64:576], w_fine)
     received(halo)
+    met(0)
+    greet(1)
     sides = dot(g.v_s1[...], g.rs1[...]).astype(BF)
     g.finx[640:672] = sides[0:32]
     g.midx[192:224] = sides[32:64]
     g.coax[64:96] = sides[64:96]
 
-    wl = g.v_wl
-    w_fine, w_mid, w_top = wl[0:C], wl[C : 2 * C], wl[2 * C : 3 * C]
     g.topb[0:96] = dot(g.coax[0:96], w_top).astype(BF)
-    g.midb[0:224] = (dot(g.midx[...], w_mid) + dot(g.v_u1[...], g.topb[...])).astype(BF)
-    g.fex[...] = dot(g.finx[...], w_fine) + dot(g.v_u2[...], g.midb[...])
+    g.midb[0:224] = (dot(g.midx[0:224], w_mid) + dot(g.v_u1[...], g.topb[...])).astype(BF)
+    fex[0:64] = dot(g.finx[0:64], w_fine)
+    fex[576:672] = dot(g.finx[576:672], w_fine)
+    fex[...] += dot(g.v_u2[...], g.midb[...])
 
     keep_n, keep_s = (1 - e_n).astype(F32), (1 - e_s).astype(F32)
     keep_w, keep_e = (1 - e_w).astype(F32), (1 - e_e).astype(F32)
@@ -299,7 +341,6 @@
             at = 9 - b if flip else 7 + b
             out[:, b * C : (b + 1) * C] = s[:, at : at + 64].astype(BF).reshape(640, C)
 
-    fex = g.fex
     spread(fex[0:64], fex[64:576], fex[576:640], fex[640:656], fex[656:672], g.fsh, False)
 
     load_wo.wait()
@@ -317,6 +358,8 @@
         return carry
 
     lax.fori_loop(0, 8, activate, 0)
+    g.xm[...] = dot(g.v_a1[...], g.midx[...]).astype(BF)
+    g.xc[...] = dot(g.v_a2[...], g.coax[...]).astype(BF)
     stores = []
 
     def store(src, dst):
@@ -339,6 +382,32 @@
         term = dot(dpre_t, fsh[64 * a : 64 * a + 512]).astype(BF)
         grad[:, :, :, lanes] = term.reshape(8, 2, 16, 768)
         pair.append(send(grad.at[:, other, :, lanes], got.at[:, :, lanes], partner))
+
+    def begin(buf, slots, dev):
+        out = []
+        for d in (1, 2, 3):
+            to, t = dev(d)
+            out.append(send(buf.at[t], slots.at[d - 1], to))
+        return out
+
+    def total(buf, mine, slots):
+        return buf[mine].astype(F32) + slots[0].astype(F32) + slots[1].astype(F32) + slots[2].astype(F32)
+
+    def split(mine, theirs, half, first, p, q):
+        wp, wq = p.shape[-1], q.shape[-1]
+        for n in range(8):
+            part = (mine[n, core].astype(F32) + theirs[n].astype(F32)).astype(BF)
+            for h in range(2):
+                at = half * h
+                p[2 * h + n % 2, n // 2] = part[:, at : at + wp]
+                q[n // 2, 2 * h + n % 2] = part[:, at + wp : at + wp + wq]
+
+    received(pair)
+    split(grad, got, 1152, 0, g.cp1, g.cq1)
+    cp = begin(g.cp1, g.cp1r, dev_x)
+    cq = begin(g.cq1, g.cq1r, dev_y)
+    met(1)
+    greet(2)
 
     received(halo)
     sides = dot(g.v_sf[...], g.rs2[...])
@@ -355,39 +424,36 @@
             dfine = term if dfine is None else dfine + term
     dfx = g.dfx
     dfx[64:576] = dfine.astype(BF)
+
+    lgrad, lgot = g.lgrad, g.lgot
+    dfine_t = dfx[64:576].T
+    lpair = []
+    for n, rows in enumerate((g.finx[64:576], g.xm[...], g.xc[...])):
+        lanes = pl.ds(n * C, C)
+        lgrad[:, :, :, lanes] = dot(dfine_t, rows).astype(BF).reshape(8, 2, 16, C)
+        lpair.append(send(lgrad.at[:, other, :, lanes], lgot.at[:, :, lanes], partner))
     halo = send_rows(dfx, 8, 64)
     g.pk3[...] = dot(g.v_pf[...], dfx[64:576]).astype(BF)
     halo += send_sides(g.pk3, g.rs3)
 
-    def begin(buf, slots, dev):
-        out = []
-        for d in (1, 2, 3):
-            to, t = dev(d)
-            out.append(send(buf.at[t], slots.at[d - 1], to))
-        return out
-
-    def total(buf, mine, slots):
-        return buf[mine].astype(F32) + slots[0].astype(F32) + slots[1].astype(F32) + slots[2].astype(F32)
-
-    def split(mine, theirs, half, first, p, q):
-        wp, wq = p.shape[-1], q.shape[-1]
-        for n in range(8):
-            part = (mine[n, core].astype(F32) + theirs[n].astype(F32)).astype(BF)
-            for h in range(2):
-                at = half * h
-                p[2 * h + n % 2, n // 2] = part[:, at : at + wp]
-                q[n // 2, 2 * h + n % 2] = part[:, at + wp : at + wp + wq]
-
-    received(pair)
-    split(grad, got, 1152, 0, g.cp1, g.cq1)
-    cp = begin(g.cp1, g.cp1r, dev_x)
-    cq = begin(g.cq1, g.cq1r, dev_y)
-
-    g.fgb[...] = dot_t(dfx[64:576], w_fine).astype(BF)
-    store(g.fgb, o_fine)
-    lgrad, lgot = g.lgrad, g.lgot
-    lgrad[:, :, :, 0:C] = dot(dfx[64:576].T, g.finx[64:576]).astype(BF).reshape(8, 2, 16, C)
-    lpair = [send(lgrad.at[:, other, :, pl.ds(0, C)], lgot.at[:, :, pl.ds(0, C)], partner)]
+    received(lpair)
+    split(lgrad, lgot, 384, 0, g.lp1, g.lq1)
+    lp = begin(g.lp1, g.lp1r, dev_x)
+    lq = begin(g.lq1, g.lq1r, dev_y)
+
+    received(cp)
+    g.cp2[...] = total(g.cp1, x, g.cp1r).astype(BF)
+    cp = begin(g.cp2, g.cp2r, dev_y)
+    received(cq)
+    g.cq2[...] = total(g.cq1, y, g.cq1r).astype(BF)
+    cq = begin(g.cq2, g.cq2r, dev_x)
+
+    received(lp)
+    g.lp2[...] = total(g.lp1, x, g.lp1r).astype(BF)
+    lp = begin(g.lp2, g.lp2r, dev_y)
+    received(lq)
+    g.lq2[...] = total(g.lq1, y, g.lq1r).astype(BF)
+    lq = begin(g.lq2, g.lq2r, dev_x)
 
     received(halo)
     wait(backward)
@@ -398,41 +464,11 @@
     g.pk4[...] = dot(g.v_pm0[...], dmx[32:160]).astype(BF)
     halo += send_sides(g.pk4, g.rs4)
 
-    received(cp)
-    g.cp2[...] = total(g.cp1, x, g.cp1r).astype(BF)
-    cp = begin(g.cp2, g.cp2r, dev_y)
-    received(cq)
-    g.cq2[...] = total(g.cq1, y, g.cq1r).astype(BF)
-    cq = begin(g.cq2, g.cq2r, dev_x)
-
-    g.mgb[...] = dot_t(dmx[32:160], w_mid).astype(BF)
-    store(g.mgb, o_mid)
-    lgrad[:, :, :, C : 2 * C] = dot(dmx[32:160].T, g.midx[32:160]).astype(BF).reshape(8, 2, 16, C)
-    lpair += [send(lgrad.at[:, other, :, pl.ds(C, C)], lgot.at[:, :, pl.ds(C, C)], partner)]
-
-    received(halo)
-    dmx[192:224] = dot(g.v_sm[...], g.rs4[...]).astype(BF)
-    dtop = dot(g.v_d2[...], dmx[...]).astype(BF)
-    g.cgb[...] = dot_t(dtop[0:32], w_top).astype(BF)
-    store(g.cgb, o_coa)
-    lgrad[:, :, :, 2 * C : 3 * C] = dot(dtop.T, g.coab[...]).astype(BF).reshape(8, 2, 16, C)
-    lpair += [send(lgrad.at[:, other, :, pl.ds(2 * C, C)], lgot.at[:, :, pl.ds(2 * C, C)], partner)]
-
-    received(lpair)
-    split(lgrad, lgot, 384, 0, g.lp1, g.lq1)
-    lp = begin(g.lp1, g.lp1r, dev_x)
-    lq = begin(g.lq1, g.lq1r, dev_y)
     sums = g.sums
     received(cp)
     sums[:, 0:CP] = total(g.cp2, y, g.cp2r)
     received(cq)
     sums[:, CP : CP + CQ] = total(g.cq2, x, g.cq2r)
-    received(lp)
-    g.lp2[...] = total(g.lp1, x, g.lp1r).astype(BF)
-    lp = begin(g.lp2, g.lp2r, dev_y)
-    received(lq)
-    g.lq2[...] = total(g.lq1, y, g.lq1r).astype(BF)
-    lq = begin(g.lq2, g.lq2r, dev_x)
     received(lp)
     sums[:, 1152 : 1152 + LP] = total(g.lp2, y, g.lp2r)
     received(lq)
@@ -458,25 +494,35 @@
     for n in range(16):
         conv = window(0, 1152, 72 * n)
         lat = window(1152, 384, 24 * n - 72)
-        g.z1[n % 4, n // 4] = jnp.where(lane < 72, conv, lat).astype(BF)
-    zc = begin(g.z1, g.z1r, dev_zlo)
+        g.z1[n] = jnp.where(lane < 72, conv, lat).astype(BF)
+    met(2)
+    zc = []
+    for d in range(1, 16):
+        to, t = dev_z(d)
+        zc.append(send(g.z1.at[t], g.z1r.at[d - 1], to))
+
+    g.fgb[...] = dot_t(dfx[64:576], w_fine).astype(BF)
+    store(g.fgb, o_fine)
+    g.mgb[...] = dot_t(dmx[32:160], w_mid).astype(BF)
+    store(g.mgb, o_mid)
+    received(halo)
+    dmx[192:224] = dot(g.v_sm[...], g.rs4[...]).astype(BF)
+    dtop = dot(g.v_d2[...], dmx[...]).astype(BF)
+    g.cgb[...] = dot_t(dtop[0:32], w_top).astype(BF)
+    store(g.cgb, o_coa)
+
     received(zc)
-    g.z2[...] = total(g.z1, z_lo, g.z1r).astype(BF)
-    z2, fin = g.z2, g.fin_r
-    zc = [send(z2.at[z_hi], fin.at[1, 0], partner)]
-    for d in (1, 2, 3):
-        for e, k in ((0, core), (1, other)):
-            to, t = dev_zhi(d, k)
-            zc.append(send(z2.at[t], fin.at[e, d], to))
-    received(zc)
-    same = z2[z_hi].astype(F32) + sum(fin[0, d].astype(F32) for d in (1, 2, 3))
-    cross = sum(fin[1, d].astype(F32) for d in range(4))
+    same = g.z1[z].astype(F32)
+    for d in range(15):
+        same += g.z1r[d].astype(F32)
+    g.z2[...] = same.astype(BF)
+    received([send(g.z2, g.z2r, partner)])
+    cross = g.z2r[...].astype(F32)
     first = core == 0
-    rows32 = [jnp.where(first, same, cross), jnp.where(first, cross, same)]
-    g.turn[...] = jnp.concatenate(rows32 + [jnp.zeros((96, LANE), F32)], 0).T
-    turn = g.turn
-    o_conv[...] = jnp.where(first, turn[0:36, 0:32], turn[36:72, 0:32])
-    o_lat[...] = jnp.where(first, turn[72:84, 0:32], turn[84:96, 0:32])
+    both = jnp.concatenate([jnp.where(first, same, cross), jnp.where(first, cross, same)], 0)
+    o_conv[...] = jnp.where(first, both[:, 0:36], pltpu.roll(both, LANE - 36, 1)[:, 0:36])
+    g.turn[...] = jnp.concatenate([both, jnp.zeros((96, LANE), F32)], 0).T
+    o_lat[...] = jnp.where(first, g.turn[72:84, 0:32], g.turn[84:96, 0:32])
 
     for copy in sent:
         copy.wait_send()
@@ -487,8 +533,8 @@
 DMA = pltpu.SemaphoreType.DMA
 SCRATCH = dict(
     finx=VM((672, C), BF),
-    midx=VM((224, C), BF),
-    coax=VM((96, C), BF),
+    midx=VM((256, C), BF),
+    coax=VM((128, C), BF),
     coab=VM((128, C), BF),
     v_wl=VM((768, C), BF),
     v_wo=VM((2304, C), BF),
@@ -547,16 +593,30 @@
     lq2=VM((4, 16, LQ), BF),
     lq2r=VM((3, 16, LQ), BF),
     sums=VM((16, 1536), F32),
-    z1=VM((4, 4, 16, LANE), BF),
-    z1r=VM((3, 4, 16, LANE), BF),
-    z2=VM((4, 16, LANE), BF),
-    fin_r=VM((2, 4, 16, LANE), BF),
+    z1=VM((16, 16, LANE), BF),
+    z1r=VM((15, 16, LANE), BF),
+    z2=VM((16, LANE), BF),
+    z2r=VM((16, LANE), BF),
+    far=pltpu.SemaphoreType.REGULAR((3,)),
+    v_a1=VM((512, 256), BF),
+    v_a2=VM((512, 128), BF),
+    xm=VM((512, C), BF),
+    xc=VM((512, C), BF),
     turn=VM((128, 128), F32),
-    lsem=DMA((20,)),
+    lsem=DMA((24,)),
     osem=DMA((4,)),
-    ssem=DMA((80,)),
-    rsem=DMA((80,)),
+    ssem=DMA((96,)),
+    rsem=DMA((96,)),
 )
+
+
+def hand_on(*refs):
+    n = len(refs) // 2
+    copies = [pltpu.make_async_copy(refs[i], refs[n + i], refs[2 * n].at[i]) for i in range(n)]
+    for copy in copies:
+        copy.start()
+    for copy in copies:
+        copy.wait()
 
 
 def local(consts, fine_in, mid_in, coarse_in, lateral_weight, out_weight, cotangent):
@@ -575,23 +635,31 @@
             jax.ShapeDtypeStruct((128, C), BF),
             jax.ShapeDtypeStruct((32, C), BF),
             jax.ShapeDtypeStruct((12, 32), F32),
-            jax.ShapeDtypeStruct((36, 32), F32),
+            jax.ShapeDtypeStruct((32, 36), F32),
         ],
         in_specs=[hbm] * len(args),
         out_specs=[hbm] * 4 + [vmem] * 2,
         scratch_shapes=list(SCRATCH.values()),
         compiler_params=pltpu.CompilerParams(
-            collective_id=0, has_side_effects=True, vmem_limit_bytes=40 * 2**20
+            collective_id=0, has_side_effects=True, vmem_limit_bytes=63 * 2**20
         ),
         cost_estimate=pl.CostEstimate(flops=2_400_000_000, bytes_accessed=4_000_000, transcendentals=262144),
     )(*args)
+    outs = pl.pallas_call(
+        hand_on,
+        out_shape=[jax.ShapeDtypeStruct(v.shape, v.dtype) for v in outs],
+        in_specs=[hbm] * len(outs),
+        out_specs=[hbm] * len(outs),
+        scratch_shapes=[pltpu.SemaphoreType.DMA((len(outs),))],
+        compiler_params=pltpu.CompilerParams(vmem_limit_bytes=63 * 2**20),
+    )(*outs)
     return (
         outs[0].reshape(fine_in.shape),
         outs[1].reshape(fine_in.shape),
         outs[2].reshape(mid_in.shape),
         outs[3].reshape(coarse_in.shape),
         outs[4],
-        outs[5],
+        outs[5].T,
     )
 
 

time: 86 us -> 71.9 us (0.84)
  local copies, waits for them, and re-layouts: 20.1 us -> 0 us
  Pallas kernels: 64.4 us -> 71.1 us
    pallas_call x0 -> x1, Pallas kernels: none -> 20.2 us  [local(): pl.pallas_call(hand_on, out_shape=[jax.ShapeDtypeStruct(v.shape, v.dtype)...]
    unnamed x40 -> x0, local copies, waits for them, and re-layouts: 20.1 us -> none
    pallas_call x1, Pallas kernels: 64.4 us -> 50.9 us  [local(): pl.pallas_call(functools.partial(kernel, tuple(consts)), out_shape=[jax.S...]
where the time goes in v2:
time: 71.9 us; the launch traced here: 71.7 us
  Pallas kernels  71.1 us (99%)
    pallas_call x1, Pallas kernels, local(): pl.pallas_call(functools.partial(kernel, tuple(consts)), out_shape=[jax.S...  50.9 us
    pallas_call x1, Pallas kernels, local(): pl.pallas_call(hand_on, out_shape=[jax.ShapeDtypeStruct(v.shape, v.dtype)...  20.2 us

profile of v2, /device:TPU:1, one launch (start us, length us, event | category | flops | bytes accessed | tf_op | source)
XLA Modules:
  0.0 71.7 jit_solution(18018138827189927942)
XLA Ops:
  0.6 50.9 %shard_map.226 = (bf16[512,256]{1,0:T(8,128)(2,1)}, bf16[512,256]{1,0:T(8,128)(2,1)}, bf16[128,256]{1,0:T(8,128)(2,1)}, bf16[32,256]{1,0:T(8,128)(2,1)}, f32[12,32]{1,0:T(8,128)}, /*index=5*/f32[32,36]{1,0:T(8,128)}) custom-call(bf16[512,256]{1,0:T(8,128)(2,1)} %bitcast.9, bf16[128,256]{1,0:T(8,128)(2,1)} %bitcast.11, bf16[32,256]{1,0:T(8,128)(2,1)} %bitcast.12, ...), custom_call_target="tpu_custom_call" | custom-call | flops 2400000000 | bytes 4000000 | tf_op jit(solution)/shard_map/pallas_call | solution.py:630
  51.5 20.2 %shard_map.227 = (bf16[512,256]{1,0:T(8,128)(2,1)}, bf16[512,256]{1,0:T(8,128)(2,1)}, bf16[128,256]{1,0:T(8,128)(2,1)}, bf16[32,256]{1,0:T(8,128)(2,1)}, f32[12,32]{1,0:T(8,128)}, /*index=5*/f32[32,36]{1,0:T(8,128)}) custom-call(bf16[512,256]{1,0:T(8,128)(2,1)} %get-tuple-element.18.refs_0_, bf16[512,256]{1,0:T(8,128)(2,1)} %get-tuple-element.19.refs_1_, ...), custom_call_target="tpu_custom_call" | custom-call | tf_op jit(solution)/shard_map/pallas_call | solution.py:648

commit v3 on v2

--- a/solution.py
+++ b/solution.py
@@ -611,11 +611,16 @@
 
 
 def hand_on(*refs):
-    n = len(refs) // 2
-    copies = [pltpu.make_async_copy(refs[i], refs[n + i], refs[2 * n].at[i]) for i in range(n)]
-    for copy in copies:
+    n = len(refs) // 3
+    ins, outs, held, sems = refs[:n], refs[n : 2 * n], refs[2 * n : 3 * n], refs[3 * n]
+    arrive = [pltpu.make_async_copy(ins[i], held[i], sems.at[0, i]) for i in range(n)]
+    leave = [pltpu.make_async_copy(held[i], outs[i], sems.at[1, i]) for i in range(n)]
+    for copy in arrive:
         copy.start()
-    for copy in copies:
+    for i in reversed(range(n)):
+        arrive[i].wait()
+        leave[i].start()
+    for copy in leave:
         copy.wait()
 
 
@@ -650,7 +655,7 @@
         out_shape=[jax.ShapeDtypeStruct(v.shape, v.dtype) for v in outs],
         in_specs=[hbm] * len(outs),
         out_specs=[hbm] * len(outs),
-        scratch_shapes=[pltpu.SemaphoreType.DMA((len(outs),))],
+        scratch_shapes=[VM(v.shape, v.dtype) for v in outs] + [DMA((2, len(outs)))],
         compiler_params=pltpu.CompilerParams(vmem_limit_bytes=63 * 2**20),
     )(*outs)
     return (

time: 71.9 us -> 53.6 us (0.75)
  Pallas kernels: 71.1 us -> 52.8 us
    pallas_call x1, Pallas kernels: 20.2 us -> 1.93 us  [local(): pl.pallas_call(hand_on, out_shape=[jax.ShapeDtypeStruct(v.shape, v.dtype)...]
where the time goes in v3:
time: 53.6 us; the launch traced here: 53.5 us
  Pallas kernels  52.8 us (99%)
  between operations  0.64 us (1%)
    pallas_call x1, Pallas kernels, local(): pl.pallas_call(functools.partial(kernel, tuple(consts)), out_shape=[jax.S...  50.9 us
    pallas_call x1, Pallas kernels, local(): pl.pallas_call(hand_on, out_shape=[jax.ShapeDtypeStruct(v.shape, v.dtype)...  1.93 us

profile of v3, /device:TPU:1, one launch (start us, length us, event | category | flops | bytes accessed | tf_op | source)
XLA Modules:
  0.0 53.5 jit_solution(9640437638647910764)
XLA Ops:
  0.6 50.9 %shard_map.226 = (bf16[512,256]{1,0:T(8,128)(2,1)}, bf16[512,256]{1,0:T(8,128)(2,1)}, bf16[128,256]{1,0:T(8,128)(2,1)}, bf16[32,256]{1,0:T(8,128)(2,1)}, f32[12,32]{1,0:T(8,128)}, /*index=5*/f32[32,36]{1,0:T(8,128)}) custom-call(bf16[512,256]{1,0:T(8,128)(2,1)} %bitcast.9, bf16[128,256]{1,0:T(8,128)(2,1)} %bitcast.11, bf16[32,256]{1,0:T(8,128)(2,1)} %bitcast.12, ...), custom_call_target="tpu_custom_call" | custom-call | flops 2400000000 | bytes 4000000 | tf_op jit(solution)/shard_map/pallas_call | solution.py:635
  51.5 1.9 %shard_map.227 = (bf16[512,256]{1,0:T(8,128)(2,1)}, bf16[512,256]{1,0:T(8,128)(2,1)}, bf16[128,256]{1,0:T(8,128)(2,1)}, bf16[32,256]{1,0:T(8,128)(2,1)}, f32[12,32]{1,0:T(8,128)}, /*index=5*/f32[32,36]{1,0:T(8,128)}) custom-call(bf16[512,256]{1,0:T(8,128)(2,1)} %get-tuple-element.18.refs_0_, bf16[512,256]{1,0:T(8,128)(2,1)} %get-tuple-element.19.refs_1_, ...), custom_call_target="tpu_custom_call" | custom-call | tf_op jit(solution)/shard_map/pallas_call | solution.py:653

commit v4 on v3

--- a/solution.py
+++ b/solution.py
@@ -57,20 +57,6 @@
                 for ci, cw in up_taps(j):
                     ri2, ci2 = clamp(ri, h, v // 3), clamp(ci, w, v % 3)
                     mat[v, place(2 * h, 2 * w, i, j), place(h, w, ri2, ci2)] += rw * cw
-    return mat.astype(ml_dtypes.bfloat16)
-
-
-def down_matrix(h, w, rows, pad):
-    mat = np.zeros((9, rows, pad), np.float32)
-    weights = (0.25, 0.75, 0.75, 0.25)
-    for v in range(9):
-        for i in range(h):
-            for j in range(w):
-                for a in range(4):
-                    for b in range(4):
-                        ri = clamp(2 * i - 1 + a, 2 * h, v // 3)
-                        ci = clamp(2 * j - 1 + b, 2 * w, v % 3)
-                        mat[v, i * w + j, place(2 * h, 2 * w, ri, ci)] += weights[a] * weights[b]
     return mat.astype(ml_dtypes.bfloat16)
 
 
@@ -86,20 +72,42 @@
     return line
 
 
-def adjoint_matrix(h, w, steps, pad):
+def adjoint_matrix(h, w, steps, rows, pad):
     fh, fw = h << steps, w << steps
-    mat = np.zeros((9, fh * fw, pad), np.float32)
+    mat = np.zeros((9, rows, pad), np.float32)
     for v in range(9):
         lines = []
         for n, kind in ((h, v // 3), (w, v % 3)):
             line = down_line(n, kind)
             for s in range(1, steps):
                 line = line[:, 1:-1] @ down_line(n << s, kind)
-            lines.append(line[:, 2:-2])
+            lines.append(line[:, 1:-1])
         both = np.multiply.outer(*lines)
-        for i in range(-1, h + 1):
-            for j in range(-1, w + 1):
-                mat[v, :, place(h, w, i, j)] = both[i + 1, :, j + 1, :].reshape(-1)
+        spots = [place(fh, fw, a, b) for a, b in cells(fh, fw)]
+        for i, j in cells(h, w):
+            mat[v, spots, place(h, w, i, j)] = both[i + 1, :, j + 1, :].reshape(-1)
+    return mat.astype(ml_dtypes.bfloat16)
+
+
+def rim_matrix():
+    mat = np.zeros((96, 512), np.float32)
+    for a in range(3):
+        for q in range(10):
+            i = q - a
+            if 0 <= i < 8:
+                mat[16 * a + q, i * 64] = 1
+                mat[48 + 16 * a + q, i * 64 + 63] = 1
+    return mat.astype(ml_dtypes.bfloat16)
+
+
+def scatter_matrix(h, w, level):
+    mat = np.zeros((h * w, 384), np.float32)
+    for side, j in ((0, 0), (1, w - 1)):
+        at = 144 * side + 16 * level
+        for i in range(h):
+            mat[i * w + j, at + 1 + i] += 1
+        mat[j, at + 48 + h + 1] += 1
+        mat[(h - 1) * w + j, at + 96] += 1
     return mat.astype(ml_dtypes.bfloat16)
 
 
@@ -128,22 +136,23 @@
         pack_matrix(8, 64, 0, 512),
         pack_matrix(4, 32, 8, 128),
         pack_matrix(2, 16, 12, 32),
-        pack_matrix(4, 32, 0, 128),
     ]
+    a1 = adjoint_matrix(4, 32, 1, 768, 256)
     return dict(
         u1=up_matrix(2, 16, 128),
         u2=up_matrix(4, 32, 256),
-        d1=down_matrix(4, 32, 128, 768),
-        d2=down_matrix(2, 16, 128, 256),
-        a1=adjoint_matrix(4, 32, 1, 256),
-        a2=adjoint_matrix(2, 16, 2, 128),
+        a1=a1,
+        a2=adjoint_matrix(2, 16, 2, 768, 128),
+        d1=np.ascontiguousarray(a1.transpose(0, 2, 1)[:, :224]),
+        d2=np.ascontiguousarray(adjoint_matrix(2, 16, 1, 256, 96).transpose(0, 2, 1)),
         pf=packs[0],
         pm=packs[1],
         pc=np.concatenate([packs[2], np.zeros((32, 96), ml_dtypes.bfloat16)], 1),
-        pm0=packs[3],
         s1=side_matrix([(8, 0), (4, 8), (2, 12)]),
-        sf=side_matrix([(8, 0)]),
-        sm=side_matrix([(4, 0)]),
+        rim=rim_matrix(),
+        tf=scatter_matrix(8, 64, 0),
+        tm=scatter_matrix(4, 32, 1),
+        tc=scatter_matrix(2, 16, 2),
     )
 
 
@@ -188,6 +197,21 @@
         return (r, x_hi * 32 + t * 2 + core), t
 
     partner = (r, x_hi * 32 + z * 2 + other)
+
+    peers = [(up, c), (down, c)] + [(a, b) for a in (r, up, down) for b in (left, right)]
+    for d in (1, 2, 3):
+        peers += [dev_x(d)[0], dev_y(d)[0]]
+    peers += [dev_z(1)[0], dev_z(15)[0]]
+    barrier = pltpu.get_barrier_semaphore()
+    for p in peers:
+        pl.semaphore_signal(barrier, inc=1, device_id=p, device_id_type=MESH)
+
+    def greet(n):
+        for d in (1 << n, 16 - (1 << n)):
+            pl.semaphore_signal(g.far.at[n], inc=1, device_id=dev_z(d)[0], device_id_type=MESH)
+
+    def met(n):
+        pl.semaphore_wait(g.far.at[n], 2)
 
     loads = []
 
@@ -211,42 +235,19 @@
         load(wl, g.v_wl),
         load(k.u1.at[variant], g.v_u1),
         load(k.u2.at[variant], g.v_u2),
-        load(k.a1.at[variant], g.v_a1),
-        load(k.a2.at[variant], g.v_a2),
     ]
-    load_wo = load(wo_hbm, g.v_wo)
-    load_cot = load(cot, g.v_cot)
-    load_sf = load(k.sf, g.v_sf)
-    backward = [
-        load(k.d1.at[variant], g.v_d1),
-        load(k.d2.at[variant], g.v_d2),
-        load(k.pm0, g.v_pm0),
-        load(k.sm, g.v_sm),
-    ]
-
     def wait(copies):
         for copy in copies:
             copy.wait()
 
-    peers = [(up, c), (down, c)] + [(a, b) for a in (r, up, down) for b in (left, right)]
-    for d in (1, 2, 3):
-        peers += [dev_x(d)[0], dev_y(d)[0]]
-    peers += [dev_z(1)[0], dev_z(15)[0]]
-    barrier = pltpu.get_barrier_semaphore()
-    for p in peers:
-        pl.semaphore_signal(barrier, inc=1, device_id=p, device_id_type=MESH)
-
-    def greet(n):
-        for d in (1 << n, 16 - (1 << n)):
-            pl.semaphore_signal(g.far.at[n], inc=1, device_id=dev_z(d)[0], device_id_type=MESH)
-
-    def met(n):
-        pl.semaphore_wait(g.far.at[n], 2)
-
-    for ref, at, count in ((g.coab, 32, 96), (g.midx, 224, 32), (g.coax, 96, 32), (g.topb, 96, 32), (g.midb, 224, 32), (g.dfx, 672, 96), (g.dmx, 224, 32)):
+    blank = ((g.coab, 32, 96), (g.midx, 224, 32), (g.coax, 96, 32), (g.topb, 96, 32), (g.midb, 224, 32))
+    blank += ((g.finx, 672, 96), (g.dfx, 672, 96), (g.dmx, 224, 32), (g.rs1, 96, 32), (g.rs2, 288, 96))
+    for ref, at, count in blank:
         ref[at : at + count] = jnp.zeros((count, C), BF)
-    for ref in (g.rs1, g.rs2, g.rs3, g.rs4):
-        ref[96:128] = jnp.zeros((32, C), BF)
+    for at in (0, 1, 10, 11):
+        g.shift0[at] = jnp.zeros((80, C), F32)
+    for at in (0, 72):
+        g.shift0[2:10, at : at + 8] = jnp.zeros((8, 8, C), F32)
 
     used = [0]
 
@@ -277,11 +278,11 @@
             send(buf.at[w * h : w * (h + 1)], buf.at[0:w], (down, c)),
         ]
 
-    def send_sides(pack, slots):
-        west, east = pack.at[0:16], pack.at[16:32]
+    def send_sides(west, east, slots):
+        count = west.shape[0]
 
         def slot(n):
-            return slots.at[16 * n : 16 * n + 16]
+            return slots.at[count * n : count * (n + 1)]
 
         return [
             send(east, slot(0), (r, right)),
@@ -298,11 +299,22 @@
     packed += dot(g.v_pc[...], g.coab[...])
     g.pk1[...] = packed.astype(BF)
     pl.semaphore_wait(barrier, len(peers))
-    halo = send_sides(g.pk1, g.rs1)
+    halo = send_sides(g.pk1.at[0:16], g.pk1.at[16:32], g.rs1)
     halo += send_rows(g.coax, 2, 16)
     halo += send_rows(g.midx, 4, 32)
     halo += send_rows(g.finx, 8, 64)
     greet(0)
+    load_wo = load(wo_hbm, g.v_wo)
+    load_cot = load(cot, g.v_cot)
+    adjoint = [load(k.a1.at[variant], g.v_a1), load(k.a2.at[variant], g.v_a2)]
+    backward = [load(k.rim, g.v_rim)]
+    closing = [
+        load(k.d1.at[variant], g.v_d1),
+        load(k.d2.at[variant], g.v_d2),
+        load(k.tf, g.v_tf),
+        load(k.tm, g.v_tm),
+        load(k.tc, g.v_tc),
+    ]
     wait(forward)
     wl = g.v_wl
     w_fine, w_mid, w_top = wl[0:C], wl[C : 2 * C], wl[2 * C : 3 * C]
@@ -327,21 +339,20 @@
     line = lax.broadcasted_iota(jnp.int32, (16, C), 0)
     keep_rows = jnp.where(line == 0, keep_n, jnp.where(line == 9, keep_s, 1.0))
 
-    def spread(north, body, south, west, east, out, flip):
-        s = g.shift
-        s[0, 8:72] = north * keep_n
-        s[1:9, 8:72] = body.reshape(8, 64, C)
-        s[9, 8:72] = south * keep_s
-        west = west * (keep_rows * keep_w)
-        east = east * (keep_rows * keep_e)
-        for i in range(10):
-            s[i, 7:8] = west[i : i + 1]
-            s[i, 72:73] = east[i : i + 1]
+    def columns(s, at, out):
         for b in range(3):
-            at = 9 - b if flip else 7 + b
-            out[:, b * C : (b + 1) * C] = s[:, at : at + 64].astype(BF).reshape(640, C)
-
-    spread(fex[0:64], fex[64:576], fex[576:640], fex[640:656], fex[656:672], g.fsh, False)
+            out[:, b * C : (b + 1) * C] = s[:, at[b] : at[b] + 64].astype(BF).reshape(out.shape[0], C)
+
+    s = g.shift
+    s[0, 8:72] = fex[0:64] * keep_n
+    s[1:9, 8:72] = fex[64:576].reshape(8, 64, C)
+    s[9, 8:72] = fex[576:640] * keep_s
+    west = fex[640:656] * (keep_rows * keep_w)
+    east = fex[656:672] * (keep_rows * keep_e)
+    for i in range(10):
+        s[i, 7:8] = west[i : i + 1]
+        s[i, 72:73] = east[i : i + 1]
+    columns(s, (7, 8, 9), g.fsh)
 
     load_wo.wait()
     wo, fsh, dsh = g.v_wo, g.fsh, g.dsh
@@ -354,12 +365,10 @@
         half = 0.5 + 0.5 * lax.erf(v * np.float32(np.sqrt(0.5)))
         g.maskb[pl.ds(at, 64)] = (v * half).astype(BF)
         slope = half + v * (jnp.exp(-0.5 * v * v) * np.float32(1 / np.sqrt(2 * np.pi)))
-        g.dpx[pl.ds(at + 64, 64)] = (g.v_cot[pl.ds(at, 64)].astype(F32) * slope).astype(BF)
+        g.dpx[pl.ds(at, 64)] = (g.v_cot[pl.ds(at, 64)].astype(F32) * slope).astype(BF)
         return carry
 
     lax.fori_loop(0, 8, activate, 0)
-    g.xm[...] = dot(g.v_a1[...], g.midx[...]).astype(BF)
-    g.xc[...] = dot(g.v_a2[...], g.coax[...]).astype(BF)
     stores = []
 
     def store(src, dst):
@@ -369,13 +378,8 @@
 
     store(g.maskb, o_mask)
 
-    load_sf.wait()
-    halo = send_rows(g.dpx, 8, 64)
-    g.pk2[...] = dot(g.v_pf[...], g.dpx[64:576]).astype(BF)
-    halo += send_sides(g.pk2, g.rs2)
-
     grad, got = g.grad, g.got
-    dpre_t = g.dpx[64:576].T
+    dpre_t = g.dpx[...].T
     pair = []
     for a in range(3):
         lanes = pl.ds(768 * a, 768)
@@ -393,7 +397,7 @@
     def total(buf, mine, slots):
         return buf[mine].astype(F32) + slots[0].astype(F32) + slots[1].astype(F32) + slots[2].astype(F32)
 
-    def split(mine, theirs, half, first, p, q):
+    def split(mine, theirs, half, p, q):
         wp, wq = p.shape[-1], q.shape[-1]
         for n in range(8):
             part = (mine[n, core].astype(F32) + theirs[n].astype(F32)).astype(BF)
@@ -402,42 +406,67 @@
                 p[2 * h + n % 2, n // 2] = part[:, at : at + wp]
                 q[n // 2, 2 * h + n % 2] = part[:, at + wp : at + wp + wq]
 
+    s = g.shift0
+    s[2:10, 8:72] = g.dpx[...].astype(F32).reshape(8, 64, C)
+    columns(s, (9, 8, 7), dsh)
+    wait(backward)
+    g.rims[...] = dot(g.v_rim[...], g.dpx[...]).astype(BF)
+    body = west = east = None
+    for a in range(3):
+        for b in range(3):
+            block = wo[(3 * a + b) * C : (3 * a + b + 1) * C]
+            term = dot_t(dsh[64 * (2 - a) : 64 * (2 - a) + 640, b * C : (b + 1) * C], block)
+            body = term if body is None else body + term
+            if b == 0:
+                term = dot_t(g.rims[16 * a : 16 * a + 16], block)
+                west = term if west is None else west + term
+            if b == 2:
+                term = dot_t(g.rims[48 + 16 * a : 64 + 16 * a], block)
+                east = term if east is None else east + term
+    dfx = g.dfx
+    dfx[0:64] = (body[0:64] * keep_n).astype(BF)
+    dfx[64:576] = body[64:576].astype(BF)
+    dfx[576:640] = (body[576:640] * keep_s).astype(BF)
+    dfx[640:656] = (west * (keep_rows * keep_w)).astype(BF)
+    dfx[656:672] = (east * (keep_rows * keep_e)).astype(BF)
+
     received(pair)
-    split(grad, got, 1152, 0, g.cp1, g.cq1)
+    split(grad, got, 1152, g.cp1, g.cq1)
     cp = begin(g.cp1, g.cp1r, dev_x)
     cq = begin(g.cq1, g.cq1r, dev_y)
     met(1)
     greet(2)
 
-    received(halo)
-    sides = dot(g.v_sf[...], g.rs2[...])
-    dpx = g.dpx
-    spread(
-        dpx[0:64].astype(F32), dpx[64:576].astype(F32), dpx[576:640].astype(F32),
-        sides[0:16], sides[16:32], dsh, True,
-    )
-    dfine = None
-    for a in range(3):
-        for b in range(3):
-            t = 3 * a + b
-            term = dot_t(dsh[64 * (2 - a) : 64 * (2 - a) + 512, b * C : (b + 1) * C], wo[t * C : (t + 1) * C])
-            dfine = term if dfine is None else dfine + term
-    dfx = g.dfx
-    dfx[64:576] = dfine.astype(BF)
-
     lgrad, lgot = g.lgrad, g.lgot
-    dfine_t = dfx[64:576].T
+    wait(adjoint)
+    dfine_t = dfx[...].T
     lpair = []
-    for n, rows in enumerate((g.finx[64:576], g.xm[...], g.xc[...])):
+    for n in range(3):
         lanes = pl.ds(n * C, C)
+        if n == 0:
+            rows = g.finx[...]
+        elif n == 1:
+            rows = dot(g.v_a1[...], g.midx[...]).astype(BF)
+        else:
+            rows = dot(g.v_a2[...], g.coax[...]).astype(BF)
         lgrad[:, :, :, lanes] = dot(dfine_t, rows).astype(BF).reshape(8, 2, 16, C)
         lpair.append(send(lgrad.at[:, other, :, lanes], lgot.at[:, :, lanes], partner))
-    halo = send_rows(dfx, 8, 64)
-    g.pk3[...] = dot(g.v_pf[...], dfx[64:576]).astype(BF)
-    halo += send_sides(g.pk3, g.rs3)
+
+    wait(closing)
+    dmx, dtx = g.dmx, g.dtx
+    dmx[0:224] = dot(g.v_d1[...], dfx[...]).astype(BF)
+    dtx[...] = dot(g.v_d2[...], dmx[...]).astype(BF)
+    north, south, west, east = g.rows_n, g.rows_s, g.cols_w, g.cols_e
+    for n, (buf, h, w, at) in enumerate(((dfx, 8, 64, 0), (dmx, 4, 32, 64), (dtx, 2, 16, 96))):
+        north[at : at + w] = buf[0:w]
+        south[at : at + w] = buf[w * (h + 1) : w * (h + 2)]
+        west[16 * n : 16 * n + 16] = buf[w * (h + 2) : w * (h + 2) + 16]
+        east[16 * n : 16 * n + 16] = buf[w * (h + 2) + 16 : w * (h + 2) + 32]
+    halo = send_sides(west, east, g.rs2)
+    halo += [send(north, g.from_s, (up, c)), send(south, g.from_n, (down, c))]
 
     received(lpair)
-    split(lgrad, lgot, 384, 0, g.lp1, g.lq1)
+    split(lgrad, lgot, 384, g.lp1, g.lq1)
     lp = begin(g.lp1, g.lp1r, dev_x)
     lq = begin(g.lq1, g.lq1r, dev_y)
 
@@ -454,15 +483,6 @@
     received(lq)
     g.lq2[...] = total(g.lq1, y, g.lq1r).astype(BF)
     lq = begin(g.lq2, g.lq2r, dev_x)
-
-    received(halo)
-    wait(backward)
-    dfx[640:672] = dot(g.v_sf[...], g.rs3[...]).astype(BF)
-    dmx = g.dmx
-    dmx[32:160] = dot(g.v_d1[...], dfx[...]).astype(BF)
-    halo = send_rows(dmx, 4, 32)
-    g.pk4[...] = dot(g.v_pm0[...], dmx[32:160]).astype(BF)
-    halo += send_sides(g.pk4, g.rs4)
 
     sums = g.sums
     received(cp)
@@ -497,19 +517,26 @@
         g.z1[n] = jnp.where(lane < 72, conv, lat).astype(BF)
     met(2)
     zc = []
-    for d in range(1, 16):
+    for d in sorted(range(1, 16), key=lambda v: abs(v - 8)):
         to, t = dev_z(d)
         zc.append(send(g.z1.at[t], g.z1r.at[d - 1], to))
 
-    g.fgb[...] = dot_t(dfx[64:576], w_fine).astype(BF)
-    store(g.fgb, o_fine)
-    g.mgb[...] = dot_t(dmx[32:160], w_mid).astype(BF)
-    store(g.mgb, o_mid)
     received(halo)
-    dmx[192:224] = dot(g.v_sm[...], g.rs4[...]).astype(BF)
-    dtop = dot(g.v_d2[...], dmx[...]).astype(BF)
-    g.cgb[...] = dot_t(dtop[0:32], w_top).astype(BF)
-    store(g.cgb, o_coa)
+    levels = (
+        (dfx, 8, 64, 0, g.v_tf, w_fine, g.fgb, o_fine),
+        (dmx, 4, 32, 64, g.v_tm, w_mid, g.mgb, o_mid),
+        (dtx, 2, 16, 96, g.v_tc, w_top, g.cgb, o_coa),
+    )
+    for buf, h, w, at, spots, weight, out, dst in levels:
+        field = buf[w : w * (h + 1)].astype(F32) + dot(spots[...], g.rs2[...])
+        rows = [
+            field[0:w] + g.from_n[at : at + w].astype(F32),
+            field[w : w * (h - 1)],
+            field[w * (h - 1) :] + g.from_s[at : at + w].astype(F32),
+        ]
+        whole = jnp.concatenate([part for part in rows if part.shape[0]], 0).astype(BF)
+        out[...] = dot_t(whole, weight).astype(BF)
+        store(out, dst)
 
     received(zc)
     same = g.z1[z].astype(F32)
@@ -532,7 +559,7 @@
 VM = pltpu.VMEM
 DMA = pltpu.SemaphoreType.DMA
 SCRATCH = dict(
-    finx=VM((672, C), BF),
+    finx=VM((768, C), BF),
     midx=VM((256, C), BF),
     coax=VM((128, C), BF),
     coab=VM((128, C), BF),
@@ -541,37 +568,42 @@
     v_cot=VM((512, C), BF),
     v_u1=VM((224, 128), BF),
     v_u2=VM((672, 256), BF),
-    v_d1=VM((128, 768), BF),
-    v_d2=VM((128, 256), BF),
+    v_d1=VM((224, 768), BF),
+    v_d2=VM((96, 256), BF),
     v_pf=VM((32, 512), BF),
     v_pm=VM((32, 128), BF),
     v_pc=VM((32, 128), BF),
-    v_pm0=VM((32, 128), BF),
     v_s1=VM((96, 128), BF),
-    v_sf=VM((32, 128), BF),
-    v_sm=VM((32, 128), BF),
     topb=VM((128, C), BF),
     midb=VM((256, C), BF),
     fex=VM((672, C), F32),
     shift=VM((10, 80, C), F32),
     fsh=VM((640, 768), BF),
-    dsh=VM((640, 768), BF),
+    dsh=VM((768, 768), BF),
+    shift0=VM((12, 80, C), F32),
+    rims=VM((96, C), BF),
+    dtx=VM((96, C), BF),
+    rows_n=VM((112, C), BF),
+    rows_s=VM((112, C), BF),
+    from_n=VM((112, C), BF),
+    from_s=VM((112, C), BF),
+    cols_w=VM((48, C), BF),
+    cols_e=VM((48, C), BF),
+    v_rim=VM((96, 512), BF),
+    v_tf=VM((512, 384), BF),
+    v_tm=VM((128, 384), BF),
+    v_tc=VM((32, 384), BF),
     pre=VM((512, C), F32),
     maskb=VM((512, C), BF),
-    dpx=VM((640, C), BF),
+    dpx=VM((512, C), BF),
     dfx=VM((768, C), BF),
     dmx=VM((256, C), BF),
     fgb=VM((512, C), BF),
     mgb=VM((128, C), BF),
     cgb=VM((32, C), BF),
     pk1=VM((32, C), BF),
-    pk2=VM((32, C), BF),
-    pk3=VM((32, C), BF),
-    pk4=VM((32, C), BF),
     rs1=VM((128, C), BF),
-    rs2=VM((128, C), BF),
-    rs3=VM((128, C), BF),
-    rs4=VM((128, C), BF),
+    rs2=VM((384, C), BF),
     grad=VM((8, 2, 16, 2304), BF),
     got=VM((8, 16, 2304), BF),
     lgrad=VM((8, 2, 16, 768), BF),
@@ -598,10 +630,8 @@
     z2=VM((16, LANE), BF),
     z2r=VM((16, LANE), BF),
     far=pltpu.SemaphoreType.REGULAR((3,)),
-    v_a1=VM((512, 256), BF),
-    v_a2=VM((512, 128), BF),
-    xm=VM((512, C), BF),
-    xc=VM((512, C), BF),
+    v_a1=VM((768, 256), BF),
+    v_a2=VM((768, 128), BF),
     turn=VM((128, 128), F32),
     lsem=DMA((24,)),
     osem=DMA((4,)),

time: 53.6 us -> 55.7 us (1.039)
  Pallas kernels: 52.8 us -> 54.9 us
    pallas_call x1, Pallas kernels: 50.9 us -> 53 us  [local(): pl.pallas_call(functools.partial(kernel, tuple(consts)), out_shape=[jax.S...]
where the time goes in v4:
time: 55.7 us; the launch traced here: 55.5 us
  Pallas kernels  54.9 us (99%)
  between operations  0.64 us (1%)
    pallas_call x1, Pallas kernels, local(): pl.pallas_call(functools.partial(kernel, tuple(consts)), out_shape=[jax.S...  53 us
    pallas_call x1, Pallas kernels, local(): pl.pallas_call(hand_on, out_shape=[jax.ShapeDtypeStruct(v.shape, v.dtype)...  1.93 us

profile of v4, /device:TPU:1, one launch (start us, length us, event | category | flops | bytes accessed | tf_op | source)
XLA Modules:
  0.0 55.5 jit_solution(6826588864618238454)
XLA Ops:
  0.6 53.0 %shard_map.235 = (bf16[512,256]{1,0:T(8,128)(2,1)}, bf16[512,256]{1,0:T(8,128)(2,1)}, bf16[128,256]{1,0:T(8,128)(2,1)}, bf16[32,256]{1,0:T(8,128)(2,1)}, f32[12,32]{1,0:T(8,128)}, /*index=5*/f32[32,36]{1,0:T(8,128)}) custom-call(bf16[512,256]{1,0:T(8,128)(2,1)} %bitcast.9, bf16[128,256]{1,0:T(8,128)(2,1)} %bitcast.11, bf16[32,256]{1,0:T(8,128)(2,1)} %bitcast.12, ...), custom_call_target="tpu_custom_call" | custom-call | flops 2400000000 | bytes 4000000 | tf_op jit(solution)/shard_map/pallas_call | solution.py:665
  53.6 1.9 %shard_map.236 = (bf16[512,256]{1,0:T(8,128)(2,1)}, bf16[512,256]{1,0:T(8,128)(2,1)}, bf16[128,256]{1,0:T(8,128)(2,1)}, bf16[32,256]{1,0:T(8,128)(2,1)}, f32[12,32]{1,0:T(8,128)}, /*index=5*/f32[32,36]{1,0:T(8,128)}) custom-call(bf16[512,256]{1,0:T(8,128)(2,1)} %get-tuple-element.18.refs_0_, bf16[512,256]{1,0:T(8,128)(2,1)} %get-tuple-element.19.refs_1_, ...), custom_call_target="tpu_custom_call" | custom-call | tf_op jit(solution)/shard_map/pallas_call | solution.py:683

commit v5 on v4

--- a/solution.py
+++ b/solution.py
@@ -452,6 +452,11 @@
         lgrad[:, :, :, lanes] = dot(dfine_t, rows).astype(BF).reshape(8, 2, 16, C)
         lpair.append(send(lgrad.at[:, other, :, lanes], lgot.at[:, :, lanes], partner))
 
+    received(lpair)
+    split(lgrad, lgot, 384, g.lp1, g.lq1)
+    lp = begin(g.lp1, g.lp1r, dev_x)
+    lq = begin(g.lq1, g.lq1r, dev_y)
+
     wait(closing)
     dmx, dtx = g.dmx, g.dtx
     dmx[0:224] = dot(g.v_d1[...], dfx[...]).astype(BF)
@@ -462,14 +467,6 @@
         south[at : at + w] = buf[w * (h + 1) : w * (h + 2)]
         west[16 * n : 16 * n + 16] = buf[w * (h + 2) : w * (h + 2) + 16]
         east[16 * n : 16 * n + 16] = buf[w * (h + 2) + 16 : w * (h + 2) + 32]
-    halo = send_sides(west, east, g.rs2)
-    halo += [send(north, g.from_s, (up, c)), send(south, g.from_n, (down, c))]
-
-    received(lpair)
-    split(lgrad, lgot, 384, g.lp1, g.lq1)
-    lp = begin(g.lp1, g.lp1r, dev_x)
-    lq = begin(g.lq1, g.lq1r, dev_y)
-
     received(cp)
     g.cp2[...] = total(g.cp1, x, g.cp1r).astype(BF)
     cp = begin(g.cp2, g.cp2r, dev_y)
@@ -521,6 +518,15 @@
         to, t = dev_z(d)
         zc.append(send(g.z1.at[t], g.z1r.at[d - 1], to))
 
+    halo = send_sides(west, east, g.rs2)
+    halo += [send(north, g.from_s, (up, c)), send(south, g.from_n, (down, c))]
+
+    received(zc)
+    same = g.z1[z].astype(F32)
+    for d in range(15):
+        same += g.z1r[d].astype(F32)
+    g.z2[...] = same.astype(BF)
+    swap = [send(g.z2, g.z2r, partner)]
     received(halo)
     levels = (
         (dfx, 8, 64, 0, g.v_tf, w_fine, g.fgb, o_fine),
@@ -538,12 +544,7 @@
         out[...] = dot_t(whole, weight).astype(BF)
         store(out, dst)
 
-    received(zc)
-    same = g.z1[z].astype(F32)
-    for d in range(15):
-        same += g.z1r[d].astype(F32)
-    g.z2[...] = same.astype(BF)
-    received([send(g.z2, g.z2r, partner)])
+    received(swap)
     cross = g.z2r[...].astype(F32)
     first = core == 0
     both = jnp.concatenate([jnp.where(first, same, cross), jnp.where(first, cross, same)], 0)

time: 55.7 us -> 51.3 us (0.921)
  Pallas kernels: 54.9 us -> 50.5 us
    pallas_call x1, Pallas kernels: 53 us -> 48.5 us  [local(): pl.pallas_call(functools.partial(kernel, tuple(consts)), out_shape=[jax.S...]
where the time goes in v5:
time: 51.3 us; the launch traced here: 51.1 us
  Pallas kernels  50.5 us (98%)
  between operations  0.64 us (1%)
    pallas_call x1, Pallas kernels, local(): pl.pallas_call(functools.partial(kernel, tuple(consts)), out_shape=[jax.S...  48.5 us
    pallas_call x1, Pallas kernels, local(): pl.pallas_call(hand_on, out_shape=[jax.ShapeDtypeStruct(v.shape, v.dtype)...  1.93 us

profile of v5, /device:TPU:1, one launch (start us, length us, event | category | flops | bytes accessed | tf_op | source)
XLA Modules:
  0.0 51.1 jit_solution(1158161863334706777)
XLA Ops:
  0.6 48.5 %shard_map.235 = (bf16[512,256]{1,0:T(8,128)(2,1)}, bf16[512,256]{1,0:T(8,128)(2,1)}, bf16[128,256]{1,0:T(8,128)(2,1)}, bf16[32,256]{1,0:T(8,128)(2,1)}, f32[12,32]{1,0:T(8,128)}, /*index=5*/f32[32,36]{1,0:T(8,128)}) custom-call(bf16[512,256]{1,0:T(8,128)(2,1)} %bitcast.9, bf16[128,256]{1,0:T(8,128)(2,1)} %bitcast.11, bf16[32,256]{1,0:T(8,128)(2,1)} %bitcast.12, ...), custom_call_target="tpu_custom_call" | custom-call | flops 2400000000 | bytes 4000000 | tf_op jit(solution)/shard_map/pallas_call | solution.py:666
  49.2 1.9 %shard_map.236 = (bf16[512,256]{1,0:T(8,128)(2,1)}, bf16[512,256]{1,0:T(8,128)(2,1)}, bf16[128,256]{1,0:T(8,128)(2,1)}, bf16[32,256]{1,0:T(8,128)(2,1)}, f32[12,32]{1,0:T(8,128)}, /*index=5*/f32[32,36]{1,0:T(8,128)}) custom-call(bf16[512,256]{1,0:T(8,128)(2,1)} %get-tuple-element.18.refs_0_, bf16[512,256]{1,0:T(8,128)(2,1)} %get-tuple-element.19.refs_1_, ...), custom_call_target="tpu_custom_call" | custom-call | tf_op jit(solution)/shard_map/pallas_call | solution.py:684

commit v6 on v5

--- a/solution.py
+++ b/solution.py
@@ -198,7 +198,7 @@
 
     partner = (r, x_hi * 32 + z * 2 + other)
 
-    peers = [(up, c), (down, c)] + [(a, b) for a in (r, up, down) for b in (left, right)]
+    peers = [(a, b) for a in (up, down, r) for b in (left, right)] + [(up, c), (down, c)]
     for d in (1, 2, 3):
         peers += [dev_x(d)[0], dev_y(d)[0]]
     peers += [dev_z(1)[0], dev_z(15)[0]]
@@ -285,12 +285,12 @@
             return slots.at[count * n : count * (n + 1)]
 
         return [
-            send(east, slot(0), (r, right)),
             send(east, slot(1), (down, right)),
             send(east, slot(2), (up, right)),
-            send(west, slot(3), (r, left)),
             send(west, slot(4), (down, left)),
             send(west, slot(5), (up, left)),
+            send(east, slot(0), (r, right)),
+            send(west, slot(3), (r, left)),
         ]
 
     wait(inputs)

time: 51.3 us -> 51.2 us (level)
  no operation moved by 1% of the time
where the time goes in v6:
time: 51.2 us; the launch traced here: 51.1 us
  Pallas kernels  50.4 us (98%)
  between operations  0.64 us (1%)
    pallas_call x1, Pallas kernels, local(): pl.pallas_call(functools.partial(kernel, tuple(consts)), out_shape=[jax.S...  48.5 us
    pallas_call x1, Pallas kernels, local(): pl.pallas_call(hand_on, out_shape=[jax.ShapeDtypeStruct(v.shape, v.dtype)...  1.93 us

profile of v6, /device:TPU:1, one launch (start us, length us, event | category | flops | bytes accessed | tf_op | source)
XLA Modules:
  0.0 51.1 jit_solution(3366281461910648340)
XLA Ops:
  0.6 48.5 %shard_map.235 = (bf16[512,256]{1,0:T(8,128)(2,1)}, bf16[512,256]{1,0:T(8,128)(2,1)}, bf16[128,256]{1,0:T(8,128)(2,1)}, bf16[32,256]{1,0:T(8,128)(2,1)}, f32[12,32]{1,0:T(8,128)}, /*index=5*/f32[32,36]{1,0:T(8,128)}) custom-call(bf16[512,256]{1,0:T(8,128)(2,1)} %bitcast.9, bf16[128,256]{1,0:T(8,128)(2,1)} %bitcast.11, bf16[32,256]{1,0:T(8,128)(2,1)} %bitcast.12, ...), custom_call_target="tpu_custom_call" | custom-call | flops 2400000000 | bytes 4000000 | tf_op jit(solution)/shard_map/pallas_call | solution.py:666
  49.1 1.9 %shard_map.236 = (bf16[512,256]{1,0:T(8,128)(2,1)}, bf16[512,256]{1,0:T(8,128)(2,1)}, bf16[128,256]{1,0:T(8,128)(2,1)}, bf16[32,256]{1,0:T(8,128)(2,1)}, f32[12,32]{1,0:T(8,128)}, /*index=5*/f32[32,36]{1,0:T(8,128)}) custom-call(bf16[512,256]{1,0:T(8,128)(2,1)} %get-tuple-element.18.refs_0_, bf16[512,256]{1,0:T(8,128)(2,1)} %get-tuple-element.19.refs_1_, ...), custom_call_target="tpu_custom_call" | custom-call | tf_op jit(solution)/shard_map/pallas_call | solution.py:684
